TPU v7x, 32 devices: a whole 2x2x4 slice. The times are simulated.
32 devices in a mesh: grp: 4 (over y, core), sub: 8 (over z, x).
Axes of the slice: x: 2, y: 2, z: 4, core: 2. Of those that a mesh axis runs over, the one named last changes fastest.
Arguments:
- sources: float32 [32, 64, 4096], P(None, None, ('grp', 'sub')), may hold values from -6 to 6
- coords: float32 [3, 64, 4096], P(None, None, ('grp', 'sub')), may hold values from 0 to 2
- leaf_basis: float32 [32, 64, 4096], P(None, None, ('grp', 'sub')), may hold values from -0.75 to 0.75
- transfer: float32 [32, 32, 4096], P(None, None, ('grp', 'sub')), may hold values from -1 to 1
- send_list: int32 [256, 16], P(('grp', 'sub')), may hold values from 0 to 127
- near_list: int32 [7, 4096], P(None, ('grp', 'sub')), may hold values from 0 to 255
- near_count: int32 [4096], P(('grp', 'sub')), may hold values from 1 to 7, as said below
- far_list: int32 [16, 512], P(None, ('grp', 'sub')), may hold values from 0 to 127
- coupling: float32 [32, 32, 16, 512], P(None, None, None, ('grp', 'sub')), may hold values from -0.25 to 0.25
- group_transfer: float32 [32, 32, 512], P(None, None, ('grp', 'sub')), may hold values from -0.09375 to 0.09375
- group_coupling: float32 [32, 32, 4, 4], replicated, may hold values from -1 to 1
Outputs:
- potential: float32 [32, 64, 4096], P(None, None, ('grp', 'sub'))
Inputs may be any that keep to these rules, and one draw needn't show every extreme that they name: `near_count`: every device holds a leaf with 7 live entries; the fewest live entries differ from device to device.
All inputs are finite; a program needn't handle non-finite values.
Results may differ from a plain program's by a relative error of at most 0.0003.
Values sent between devices are 32-bit elements; how exact they have to be, the bound alone decides.
A program may use at most 192 MiB of HBM per device.

v0:
```python
import math

import jax
import jax.numpy as jnp
from jax import lax
from jax.experimental import pallas as pl
from jax.experimental.pallas import tpu as pltpu
from jax.sharding import PartitionSpec as P

INV_FOUR_PI = 1.0 / (4.0 * math.pi)
EPS_SQ = 0.01
HIGH = lax.Precision.HIGHEST
MESH = pl.DeviceIdType.MESH
LANES = 128
CHILDREN = 8


def mm(a, b, dims=((1,), (0,))):
    return lax.dot_general(a, b, (dims, ((), ())), precision=HIGH, preferred_element_type=jnp.float32)


def lane_block(rows):
    return lax.broadcasted_iota(jnp.int32, (rows, LANES), 1) // 32


def pick_blocks(parts):
    blk = lane_block(parts[0].shape[0])
    out = parts[3]
    for a in (2, 1, 0):
        out = jnp.where(blk == a, parts[a], out)
    return out


def fold(full):
    y = pick_blocks([full[32 * a:32 * a + 32] for a in range(4)])
    y = y + pltpu.roll(y, 64, 1)
    return y + pltpu.roll(y, 32, 1)


def dense(y):
    return pick_blocks([y[8 * a:8 * a + 8] for a in range(4)])


def exchange_kernel(n_grp, n_sub, par, cap,
                    send_list, far_idx, own, own_pts, basis, trans, coup, gt_up, gt_down, gcoup,
                    recv, far,
                    send, ps_all, gs_all, field, send_sem, recv_sem, ps_send, ps_recv, gs_send, gs_recv):
    me = lax.axis_index("sub")
    grp = lax.axis_index("grp")
    barrier = pltpu.get_barrier_semaphore()
    for o in range(1, n_sub):
        pl.semaphore_signal(barrier, inc=1, device_id={"sub": lax.rem(me + o, n_sub)}, device_id_type=MESH)
    for o in range(1, n_grp):
        pl.semaphore_signal(barrier, inc=1, device_id={"grp": lax.rem(grp + o, n_grp)}, device_id_type=MESH)

    left = lax.broadcasted_iota(jnp.int32, (16, LANES), 1) < 64
    left8 = lax.broadcasted_iota(jnp.int32, (8, LANES), 1) < 64

    def pack(peer, carry):
        tops = []
        for s in range(cap):
            leaf = send_list[peer, s]
            block = own[leaf]
            send[peer, 16 * s:16 * s + 16, :] = jnp.where(left, block[:16], block[16:])
            tops.append(own_pts[leaf])
        for p in range(cap // 2):
            both = jnp.where(left8, tops[2 * p], tops[2 * p + 1])
            for d in range(3):
                row = 16 * cap + (cap // 2) * d + p
                send[peer, row:row + 1, :] = both[d:d + 1]
        return carry

    lax.fori_loop(0, n_sub, pack, 0)
    pl.semaphore_wait(barrier, n_sub - 1 + n_grp - 1)

    def value_copy(o):
        peer = lax.rem(me + o, n_sub)
        return pltpu.make_async_remote_copy(
            src_ref=send.at[peer], dst_ref=recv.at[me], send_sem=send_sem.at[o], recv_sem=recv_sem.at[o],
            device_id={"sub": peer}, device_id_type=MESH)

    for o in range(1, n_sub):
        value_copy(o).start()
    recv[me] = send[me]

    same = (lax.broadcasted_iota(jnp.int32, (256, 256), 0) // 32
            == lax.broadcasted_iota(jnp.int32, (256, 256), 1) // 32)

    def lift(c, carry):
        first = pl.multiple_of(c * CHILDREN, CHILDREN)
        rows = pl.ds(pl.multiple_of(c * 256, 256), 256)
        vals = own[pl.ds(first, CHILDREN)].reshape(256, LANES)[:, :64]
        skel = jnp.where(same, mm(basis[rows, :], vals, ((1,), (1,))), 0.0)
        up = mm(trans[rows, :], skel, ((0,), (0,)))
        y = up[:, :LANES] + up[:, LANES:]
        y = y + pltpu.roll(y, 64, 1)
        y = y + pltpu.roll(y, 32, 1)
        ps_all[me * (par + 1) + c] = dense(y)
        return carry

    lax.fori_loop(0, par, lift, 0)
    mine = ps_all[pl.ds(me * (par + 1), par)].reshape(par * 8, LANES)
    ps_all[me * (par + 1) + par] = dense(fold(mm(gt_up[...], mine)))

    def skel_copy(o):
        part = ps_all.at[pl.ds(me * (par + 1), par + 1)]
        return pltpu.make_async_remote_copy(
            src_ref=part, dst_ref=part, send_sem=ps_send.at[o], recv_sem=ps_recv.at[o],
            device_id={"sub": lax.rem(me + o, n_sub)}, device_id_type=MESH)

    for o in range(1, n_sub):
        skel_copy(o).start()
    for o in range(1, n_sub):
        skel_copy(o).wait()

    total = ps_all[par]
    for m in range(1, n_sub):
        total = total + ps_all[m * (par + 1) + par]
    gs_all[grp] = total

    def group_copy(o):
        return pltpu.make_async_remote_copy(
            src_ref=gs_all.at[grp], dst_ref=gs_all.at[grp], send_sem=gs_send.at[o], recv_sem=gs_recv.at[o],
            device_id={"grp": lax.rem(grp + o, n_grp)}, device_id_type=MESH)

    for o in range(1, n_grp):
        group_copy(o).start()

    def local(c, carry):
        partners = jnp.concatenate([ps_all[far_idx[f, c]] for f in range(16)], axis=0)
        field[c] = fold(mm(coup[c], partners))
        return carry

    lax.fori_loop(0, par, local, 0)
    for o in range(1, n_grp):
        group_copy(o).wait()
    inflow = fold(mm(gcoup[...], gs_all[...].reshape(n_grp * 8, LANES)))

    def down(c, carry):
        rows = pl.ds(pl.multiple_of(c * 256, 256), 256)
        here = field[c] + mm(gt_down[pl.ds(pl.multiple_of(c * 32, 32), 32), :], inflow)
        leaf_field = mm(here.T, trans[rows, :], ((1,), (1,)))
        spread = jnp.where(same, jnp.concatenate([leaf_field, leaf_field], axis=0), 0.0)
        far[rows, :] = mm(spread, basis[rows, :])
        return carry

    lax.fori_loop(0, par, down, 0)
    for o in range(1, n_sub):
        value_copy(o).wait()


def near_kernel(n_sub, cap, slots, leaves, idx, own, own_pts, recv, far, out, vals, pts):
    left8 = lax.broadcasted_iota(jnp.int32, (8, LANES), 1) < 64
    left16 = lax.broadcasted_iota(jnp.int32, (16, LANES), 1) < 64
    left64 = lax.broadcasted_iota(jnp.int32, (64, LANES), 1) < 64

    def put(slot, block):
        high = block.astype(jnp.bfloat16)
        vals[slot, 0:32, :] = high
        vals[slot, 32:64, :] = (block - high.astype(jnp.float32)).astype(jnp.bfloat16)

    def keep(l, carry):
        put(l, own[l])
        pts[l] = own_pts[l]
        return carry

    lax.fori_loop(0, leaves, keep, 0, unroll=8)

    def unpack(peer, carry):
        base = leaves + peer * cap
        for s in range(cap):
            d = recv[peer, 16 * s:16 * s + 16, :]
            turned = pltpu.roll(d, 64, 1)
            put(base + s, jnp.concatenate([jnp.where(left16, d, turned), jnp.where(left16, turned, d)], axis=0))
        for d in range(3):
            start = 16 * cap + (cap // 2) * d
            tile = recv[peer, start:start + cap // 2, :]
            turned = pltpu.roll(tile, 64, 1)
            even, odd = jnp.where(left8, tile, turned), jnp.where(left8, turned, tile)
            for p in range(cap // 2):
                pts[base + 2 * p, d:d + 1, :] = even[p:p + 1]
                pts[base + 2 * p + 1, d:d + 1, :] = odd[p:p + 1]
        return carry

    lax.fori_loop(0, n_sub, unpack, 0)
    vals[slots] = jnp.zeros((64, LANES), jnp.bfloat16)
    pts[slots] = jnp.zeros((8, LANES), jnp.float32)

    def one_leaf(i, carry):
        cols = own_pts[i].T
        target = [jnp.broadcast_to(cols[:64, d:d + 1], (64, LANES)) for d in range(3)]
        values, highs, lows = [], [], []
        for p in range(4):
            a, b = idx[2 * p, i], idx[2 * p + 1, i]
            points = jnp.where(left8, pts[a], pts[b])
            values.append(jnp.where(left64, vals[a], vals[b]))
            dist = EPS_SQ
            for d in range(3):
                diff = target[d] - points[d:d + 1, :]
                dist = dist + diff * diff
            kern = lax.rsqrt(dist)
            high = kern.astype(jnp.bfloat16)
            highs.append(high)
            lows.append((kern - high.astype(jnp.float32)).astype(jnp.bfloat16))
        v = jnp.concatenate(values, axis=1)
        nt = (((1,), (1,)), ((), ()))
        main = lax.dot_general(v, jnp.concatenate(highs, axis=1), nt, preferred_element_type=jnp.float32)
        rest = lax.dot_general(v[:32], jnp.concatenate(lows, axis=1), nt, preferred_element_type=jnp.float32)
        out[i] = far[i] + INV_FOUR_PI * (main[:32] + main[32:] + rest)
        return carry

    lax.fori_loop(0, leaves, one_leaf, 0, unroll=2)


def body(
    sources,
    coords,
    leaf_basis,
    transfer,
    send_list,
    near_list,
    near_count,
    far_list,
    coupling,
    group_transfer,
    group_coupling,
):
    n_sub = lax.axis_size("sub")
    n_grp = lax.axis_size("grp")
    leaves = sources.shape[2]
    par = leaves // CHILDREN
    cap = send_list.shape[1]
    slots = leaves + n_sub * cap
    near_entries = near_list.shape[0]
    f32 = jnp.float32

    x = jnp.transpose(sources, (2, 0, 1))
    own = jnp.concatenate([x, x], axis=2)
    y = jnp.transpose(coords, (2, 0, 1))
    own_pts = jnp.pad(jnp.concatenate([y, y], axis=2), ((0, 0), (0, 5), (0, 0)))
    basis = jnp.transpose(leaf_basis, (2, 0, 1)).reshape(leaves * 32, 64)
    trans = jnp.transpose(transfer, (2, 1, 0)).reshape(leaves * 32, 32)
    coup = coupling.reshape(32, 4, 8, 16, par).transpose(4, 1, 0, 3, 2).reshape(par, 128, 128)
    gt_up = group_transfer.reshape(32, 4, 8, par).transpose(1, 0, 3, 2).reshape(128, par * 8)
    gt_down = jnp.transpose(group_transfer, (2, 1, 0)).reshape(par * 32, 32)
    my_group = lax.axis_index("grp")
    row = lax.dynamic_index_in_dim(group_coupling, my_group, 2, keepdims=False)
    others = (jnp.arange(n_grp, dtype=jnp.int32) != my_group).astype(f32)
    gcoup = (row * others).reshape(32, 4, 8, n_grp).transpose(1, 0, 3, 2).reshape(128, n_grp * 8)
    far_idx = far_list + far_list // par
    live = jnp.arange(near_entries, dtype=jnp.int32)[:, None] < near_count[None, :]
    idx = jnp.pad(jnp.where(live, near_list, slots), ((0, 8 - near_entries), (0, 0)), constant_values=slots)

    vmem = pl.BlockSpec(memory_space=pltpu.VMEM)
    smem = pl.BlockSpec(memory_space=pltpu.SMEM)
    rows = 16 * cap + 3 * (cap // 2)
    dma = pltpu.SemaphoreType.DMA
    recv, far = pl.pallas_call(
        lambda *refs: exchange_kernel(n_grp, n_sub, par, cap, *refs),
        out_shape=(jax.ShapeDtypeStruct((n_sub, rows, LANES), f32),
                   jax.ShapeDtypeStruct((leaves * 32, 64), f32)),
        in_specs=[smem, smem] + [vmem] * 8,
        out_specs=(vmem, vmem),
        scratch_shapes=[
            pltpu.VMEM((n_sub, rows, LANES), f32),
            pltpu.VMEM((n_sub * (par + 1), 8, LANES), f32),
            pltpu.VMEM((n_grp, 8, LANES), f32),
            pltpu.VMEM((par, 32, LANES), f32),
            dma((n_sub,)), dma((n_sub,)), dma((n_sub,)), dma((n_sub,)), dma((n_grp,)), dma((n_grp,)),
        ],
        compiler_params=pltpu.CompilerParams(
            collective_id=0, has_side_effects=True, vmem_limit_bytes=48 * 2**20),
        name="exchange_far",
    )(send_list, far_idx, own, own_pts, basis, trans, coup, gt_up, gt_down, gcoup)

    out = pl.pallas_call(
        lambda *refs: near_kernel(n_sub, cap, slots, leaves, *refs),
        out_shape=jax.ShapeDtypeStruct((leaves, 32, 64), f32),
        in_specs=[smem] + [vmem] * 4,
        out_specs=vmem,
        scratch_shapes=[
            pltpu.VMEM((slots + 1, 64, LANES), jnp.bfloat16),
            pltpu.VMEM((slots + 1, 8, LANES), f32),
        ],
        compiler_params=pltpu.CompilerParams(vmem_limit_bytes=48 * 2**20),
        name="near_field",
    )(idx, own, own_pts, recv, far.reshape(leaves, 32, 64))
    return jnp.transpose(out, (1, 2, 0))


def solution(mesh):
    whole = ("grp", "sub")
    return jax.shard_map(
        body,
        mesh=mesh,
        in_specs=(
            P(None, None, whole),
            P(None, None, whole),
            P(None, None, whole),
            P(None, None, whole),
            P(whole, None),
            P(None, whole),
            P(whole),
            P(None, whole),
            P(None, None, None, whole),
            P(None, None, whole),
            P(),
        ),
        out_specs=P(None, None, whole),
        check_vma=False,
    )
```

profile of v0, /device:TPU:8, one launch (start us, length us, event | category | flops | bytes accessed | tf_op | source)
XLA Modules:
  0.0 133.6 jit_solution(12773315758731393147)
XLA Ops:
  0.0 0.0 copy-start
  0.0 0.9 copy-done
  1.0 0.1 copy.35
  1.1 0.1 fusion
  1.2 0.1 reshape.42
  1.3 0.1 copy.33.refs_9_
  1.4 3.1 %copy.20 = f32[32,64,128]{1,0,2:T(8,128)S(1)} copy(f32[32,64,128]{2,1,0:T(8,128)} %param.11) | data formatting | bytes 2097152 | tf_op args[0]
  4.4 0.0 copy-start.6
  4.4 2.0 %pad_maximum_fusion.refs_2_.refs_1_ = f32[128,32,128]{2,1,0:T(8,128)} fusion(f32[128,32,64]{2,1,0:T(8,128)S(1)} %bitcast.34), kind=kLoop, calls=%fused_computation | loop fusion | flops 524288 | bytes 3145728 | tf_op jit(solution)/shard_map/concatenate | solution.py:238
  6.4 0.0 copy-done.6
  6.4 0.1 copy.21
  6.6 0.2 select_maximum_fusion.refs_3_.refs_2_
  6.8 7.1 %copy.24 = f32[32,32,16,16]{0,3,2,1:T(8,128)} copy(f32[32,32,16,16]{1,3,2,0:T(8,128)} %param.19) | data formatting | bytes 2097152 | tf_op args[8]
  13.9 6.9 %copy.25 = f32[16,4,32,16,8]{2,1,4,3,0:T(4,128)} copy(f32[16,4,32,16,8]{2,0,3,4,1:T(8,128)} %bitcast.31) | data formatting | bytes 2097152 | tf_op jit(solution)/shard_map/transpose | solution.py:243
  20.8 3.7 %reshape.38 = f32[16,128,128]{1,2,0:T(8,128)S(1)} reshape(f32[16,4,32,16,8]{2,1,4,3,0:T(4,128)} %copy.25) | data formatting | bytes 2097152 | tf_op jit(solution)/shard_map/reshape | solution.py:243
  24.5 0.3 copy.31.refs_6_
  24.8 0.0 copy-start.5
  24.8 4.1 %copy.22 = f32[128,32,64]{2,1,0:T(8,128)} copy(f32[128,32,64]{0,2,1:T(8,128)} %bitcast.35) | data formatting | bytes 2097152 | tf_op jit(solution)/shard_map/transpose | solution.py:241
  28.9 0.0 copy-start.4
  28.9 0.0 copy-done.5
  28.9 0.0 copy-start.7
  28.9 0.0 copy-start.3
  28.9 2.9 %copy.23 = f32[128,32,32]{2,1,0:T(8,128)} copy(f32[128,32,32]{0,1,2:T(8,128)S(1)} %bitcast.39) | data formatting | bytes 1048576 | tf_op jit(solution)/shard_map/transpose | solution.py:242
  31.8 0.0 copy-done.4
  31.8 0.2 copy.26
  32.0 0.2 copy.27
  32.2 0.2 reshape.40
  32.4 0.1 copy.32.refs_7_
  32.4 0.2 copy.28
  32.6 0.0 copy-done.7
  32.6 0.0 copy-done.3
  32.7 0.0 copy-start.8
  32.7 0.0 copy-start.9
  32.7 0.0 copy-start.1
  32.7 65.5 %exchange_far.1 = (f32[8,280,128]{2,1,0:T(8,128)S(1)}, f32[4096,64]{1,0:T(8,128)S(1)}) custom-call(s32[8,16]{1,0:T(8,128)S(1)} %copy-done.3, s32[16,16]{1,0:T(8,128)S(1)} %fusion.2.refs_1_, f32[128,32,128]{2,1,0:T(8,128)} %pad_maximum_fusion.refs_2_.refs_1_, f32[128,8,128]{2,1,0:T(8,128)S(1)} %select_maximum_fusion.refs_3_.refs_2_, f32[4096,64]{1,0:T(8,128)} %bitcast.33, ...), custom_call_target="tpu_custom_call" | custom-call | tf_op jit(solution)/shard_map/exchange_far/pallas_call | solution.py:258
  98.2 0.0 copy-start.2
  98.2 1.3 copy-done.2
  99.6 0.0 copy-done.8
  99.6 0.0 copy-done.9
  99.6 0.0 copy-done.1
  99.6 31.8 %near_field.1 = f32[128,32,64]{2,1,0:T(8,128)S(1)} custom-call(s32[8,128]{1,0:T(8,128)S(1)} %pad.8.refs_0_, f32[128,32,128]{2,1,0:T(8,128)S(1)} %copy-done.1, f32[128,8,128]{2,1,0:T(8,128)S(1)} %select_maximum_fusion.refs_3_.refs_2_, f32[8,280,128]{2,1,0:T(8,128)S(1)} %get-tuple-element.7.refs_3_, f32[128,32,64]{2,1,0:T(8,128)} %bitcast.29), custom_call_target="tpu_custom_call" | custom-call | tf_op jit(solution)/shard_map/near_field/pallas_call | solution.py:276
  131.3 2.3 %copy.34 = f32[32,64,128]{2,1,0:T(8,128)} copy(f32[32,64,128]{1,0,2:T(8,128)S(1)} %bitcast.28) | data formatting | bytes 2097152 | tf_op jit(solution)/shard_map/transpose | solution.py:288
  (6 shorter events, 0.1 us)
Async XLA Ops:
  0.0 1.0 copy-start
  4.4 2.0 %copy-start.6 = (f32[3,64,128]{2,1,0:T(8,128)S(1)}, f32[3,64,128]{2,1,0:T(8,128)}, u32[]{:S(2)}) copy-start(f32[3,64,128]{2,1,0:T(8,128)} %param.12) | copy-start | bytes 294916
  24.8 4.1 %copy-start.5 = (f32[32,32,128]{2,1,0:T(8,128)S(1)}, f32[32,32,128]{2,1,0:T(8,128)}, u32[]{:S(2)}) copy-start(f32[32,32,128]{2,1,0:T(8,128)} %param.14) | copy-start | bytes 1572868
  28.9 2.9 %copy-start.4 = (f32[32,32,16]{1,2,0:T(8,128)S(1)}, f32[32,32,16]{1,2,0:T(8,128)}, u32[]{:S(2)}) copy-start(f32[32,32,16]{1,2,0:T(8,128)} %param.20) | copy-start | bytes 196612
  28.9 3.7 %copy-start.7 = (s32[16,16]{1,0:T(8,128)S(1)}, s32[16,16]{1,0:T(8,128)}, u32[]{:S(2)}) copy-start(s32[16,16]{1,0:T(8,128)} %param.18) | copy-start | bytes 3076
  28.9 3.7 %copy-start.3 = (s32[8,16]{1,0:T(8,128)S(1)}, s32[8,16]{1,0:T(8,128)}, u32[]{:S(2)}) copy-start(s32[8,16]{1,0:T(8,128)} %refs_0_.1) | copy-start | bytes 1540
  32.7 66.9 %copy-start.8 = (s32[7,128]{1,0:T(8,128)S(1)}, s32[7,128]{1,0:T(8,128)}, u32[]{:S(2)}) copy-start(s32[7,128]{1,0:T(8,128)} %param.16) | copy-start | bytes 10756
  32.7 66.9 %copy-start.9 = (s32[128]{0:T(128)S(1)}, s32[128]{0:T(128)}, u32[]{:S(2)}) copy-start(s32[128]{0:T(128)} %param.17) | copy-start | bytes 1540
  32.7 66.9 %copy-start.1 = (f32[128,32,128]{2,1,0:T(8,128)S(1)}, f32[128,32,128]{2,1,0:T(8,128)}, u32[]{:S(2)}) copy-start(f32[128,32,128]{2,1,0:T(8,128)} %pad_maximum_fusion.refs_2_.refs_1_) | copy-start | bytes 6291460
  98.2 1.3 copy-start.2
where the time goes:
time: 134 us
  Pallas kernels  97.3 us (73%)
  local copies, waits for them, and re-layouts  33.9 us (25%)
  other arithmetic  2.27 us (2%)
    pallas_call x1, Pallas kernels, body(): pl.pallas_call(lambda *refs: exchange_kernel(n_grp, n_sub, par, cap, *ref...  65.5 us
    pallas_call x1, Pallas kernels, body(): pl.pallas_call(lambda *refs: near_kernel(n_sub, cap, slots, leaves, *refs...  31.8 us
    unnamed x25, local copies, waits for them, and re-layouts  12.9 us
    transpose x1, local copies, waits for them, and re-layouts, body(): coupling.reshape(32, 4, 8, 16, par).transpose(4, 1, 0, 3, 2)  6.85 us
    transpose x1, local copies, waits for them, and re-layouts, body(): basis = jnp.transpose(leaf_basis, (2, 0, 1)).reshape(leaves * 32, 64)  4.11 us
    reshape x2, local copies, waits for them, and re-layouts, body(): coupling.reshape(32, 4, 8, 16, par).transpose(4, 1, 0, 3, 2)  4.04 us
    transpose x1, local copies, waits for them, and re-layouts, body(): trans = jnp.transpose(transfer, (2, 1, 0)).reshape(leaves * 32, 32)  2.85 us

commit v1 on v0

v1 whole, which is shorter than its diff:
```python
import math

import jax
import jax.numpy as jnp
from jax import lax
from jax.experimental import pallas as pl
from jax.experimental.pallas import tpu as pltpu
from jax.sharding import PartitionSpec as P

INV_FOUR_PI = 1.0 / (4.0 * math.pi)
EPS_SQ = 0.01
MESH = pl.DeviceIdType.MESH
LANES = 128
CHILDREN = 8


def halves(x):
    high = x.astype(jnp.bfloat16)
    return high, (x - high.astype(jnp.float32)).astype(jnp.bfloat16)


def mm(a, b, dims=((1,), (0,))):
    def dot(x, y):
        return lax.dot_general(x, y, (dims, ((), ())), preferred_element_type=jnp.float32)
    a0, a1 = halves(a)
    b0, b1 = halves(b)
    return dot(a0, b0) + (dot(a0, b1) + dot(a1, b0))


def lane_block(rows):
    return lax.broadcasted_iota(jnp.int32, (rows, LANES), 1) // 32


def pick_blocks(parts):
    blk = lane_block(parts[0].shape[0])
    out = parts[3]
    for a in (2, 1, 0):
        out = jnp.where(blk == a, parts[a], out)
    return out


def spread_lanes(y):
    y = jnp.where(lane_block(y.shape[0]) == 0, y, 0.0)
    y = y + pltpu.roll(y, 32, 1)
    return y + pltpu.roll(y, 64, 1)


def loose(block):
    return jnp.concatenate([block] + [pltpu.roll(block, LANES - 32 * a, 1) for a in range(1, 4)], axis=0)


def dense(y):
    return pick_blocks([y[8 * a:8 * a + 8] for a in range(4)])


def exchange_kernel(n_grp, n_sub, par, cap,
                    send_list, far_list, own, own_pts, basis, trans, gt, gcoup, coup_hbm,
                    recv, far,
                    send, ps_all, gs_all, loose_all, field, coup, send_sem, recv_sem, ps_send, ps_recv, gs_send,
                    gs_recv, coup_sem):
    me = lax.axis_index("sub")
    grp = lax.axis_index("grp")
    barrier = pltpu.get_barrier_semaphore()
    for o in range(1, n_sub):
        pl.semaphore_signal(barrier, inc=1, device_id={"sub": lax.rem(me + o, n_sub)}, device_id_type=MESH)
    for o in range(1, n_grp):
        pl.semaphore_signal(barrier, inc=1, device_id={"grp": lax.rem(grp + o, n_grp)}, device_id_type=MESH)

    coup_copy = pltpu.make_async_copy(coup_hbm, coup, coup_sem)
    coup_copy.start()
    same = (lax.broadcasted_iota(jnp.int32, (256, 256), 0) // 32
            == lax.broadcasted_iota(jnp.int32, (256, 256), 1) // 32)

    def lift(c, carry):
        first = pl.multiple_of(c * CHILDREN, CHILDREN)
        rows = pl.ds(pl.multiple_of(c * 256, 256), 256)
        vals = own[pl.ds(first, CHILDREN)].reshape(256, LANES)[:, :64]
        skel = jnp.where(same, mm(basis[rows, :], vals, ((1,), (1,))), 0.0)
        up = mm(trans[rows, :], skel, ((0,), (0,)))
        y = up[:, :LANES] + up[:, LANES:]
        y = y + pltpu.roll(y, 64, 1)
        y = y + pltpu.roll(y, 32, 1)
        ps_all[me * (par + 1) + c] = dense(y)
        return carry + mm(gt[pl.ds(c, 32, stride=par), :], y)

    part = lax.fori_loop(0, par, lift, jnp.zeros((32, LANES), jnp.float32))
    ps_all[me * (par + 1) + par] = dense(part)
    pl.semaphore_wait(barrier, n_sub - 1 + n_grp - 1)

    def skel_copy(o):
        part = ps_all.at[pl.ds(me * (par + 1), par + 1)]
        return pltpu.make_async_remote_copy(
            src_ref=part, dst_ref=part, send_sem=ps_send.at[o], recv_sem=ps_recv.at[o],
            device_id={"sub": lax.rem(me + o, n_sub)}, device_id_type=MESH)

    for o in range(1, n_sub):
        skel_copy(o).start()

    left = lax.broadcasted_iota(jnp.int32, (16, LANES), 1) < 64
    left8 = lax.broadcasted_iota(jnp.int32, (8, LANES), 1) < 64

    def pack(peer, carry):
        tops = []
        for s in range(cap):
            leaf = send_list[peer, s]
            block = own[leaf]
            send[peer, 16 * s:16 * s + 16, :] = jnp.where(left, block[:16], block[16:])
            tops.append(own_pts[leaf])
        for p in range(cap // 2):
            both = jnp.where(left8, tops[2 * p], tops[2 * p + 1])
            for d in range(3):
                row = 16 * cap + (cap // 2) * d + p
                send[peer, row:row + 1, :] = both[d:d + 1]
        return carry

    lax.fori_loop(0, n_sub, pack, 0)
    def value_copy(o):
        peer = lax.rem(me + o, n_sub)
        return pltpu.make_async_remote_copy(
            src_ref=send.at[peer], dst_ref=recv.at[me], send_sem=send_sem.at[o], recv_sem=recv_sem.at[o],
            device_id={"sub": peer}, device_id_type=MESH)

    for o in range(1, n_sub):
        value_copy(o).start()
    recv[me] = send[me]

    for o in range(1, n_sub):
        skel_copy(o).wait()

    total = ps_all[par]
    for m in range(1, n_sub):
        total = total + ps_all[m * (par + 1) + par]
    gs_all[grp] = total

    def group_copy(o):
        return pltpu.make_async_remote_copy(
            src_ref=gs_all.at[grp], dst_ref=gs_all.at[grp], send_sem=gs_send.at[o], recv_sem=gs_recv.at[o],
            device_id={"grp": lax.rem(grp + o, n_grp)}, device_id_type=MESH)

    for o in range(1, n_grp):
        group_copy(o).start()

    def loosen(m, carry):
        for c in range(par):
            loose_all[m * par + c] = loose(ps_all[m * (par + 1) + c])
        return carry

    lax.fori_loop(0, n_sub, loosen, 0)
    coup_copy.wait()

    def local(c, carry):
        partners = jnp.concatenate([loose_all[far_list[f, c]] for f in range(16)], axis=0)
        blocks = jnp.concatenate([coup[pl.ds(f * par + c, 32, stride=16 * par), :] for f in range(16)], axis=1)
        field[c] = spread_lanes(mm(blocks, partners))
        return carry

    lax.fori_loop(0, par, local, 0)
    for o in range(1, n_grp):
        group_copy(o).wait()
    inflow = jnp.zeros((32, LANES), jnp.float32)
    for h in range(n_grp):
        live = jnp.where(grp == h, 0.0, 1.0)
        block = gcoup[pl.ds(grp * n_grp + h, 32, stride=n_grp * n_grp), :]
        inflow = inflow + mm(block * live, loose(gs_all[h]))
    inflow = spread_lanes(inflow)

    def down(c, carry):
        rows = pl.ds(pl.multiple_of(c * 256, 256), 256)
        here = field[c] + mm(gt[pl.ds(c, 32, stride=par), :], inflow, ((0,), (0,)))
        leaf_field = mm(here.T, trans[rows, :], ((1,), (1,)))
        spread = jnp.where(same, jnp.concatenate([leaf_field, leaf_field], axis=0), 0.0)
        far[rows, :] = mm(spread, basis[rows, :])
        return carry

    lax.fori_loop(0, par, down, 0)
    for o in range(1, n_sub):
        value_copy(o).wait()


def near_kernel(n_sub, cap, slots, leaves, idx, own, own_pts, recv, far, out, vals, pts):
    left8 = lax.broadcasted_iota(jnp.int32, (8, LANES), 1) < 64
    left16 = lax.broadcasted_iota(jnp.int32, (16, LANES), 1) < 64

    def put(slot, block):
        high = block.astype(jnp.bfloat16).astype(jnp.float32)
        both = jnp.concatenate([high, block - high], axis=0)
        vals[slot] = both.T[:64].astype(jnp.bfloat16)

    def keep(l, carry):
        put(l, own[l])
        pts[l] = own_pts[l]
        return carry

    lax.fori_loop(0, leaves, keep, 0, unroll=8)

    def unpack(peer, carry):
        base = leaves + peer * cap
        for s in range(cap):
            d = recv[peer, 16 * s:16 * s + 16, :]
            turned = pltpu.roll(d, 64, 1)
            put(base + s, jnp.concatenate([jnp.where(left16, d, turned), jnp.where(left16, turned, d)], axis=0))
        for d in range(3):
            start = 16 * cap + (cap // 2) * d
            tile = recv[peer, start:start + cap // 2, :]
            turned = pltpu.roll(tile, 64, 1)
            even, odd = jnp.where(left8, tile, turned), jnp.where(left8, turned, tile)
            for p in range(cap // 2):
                pts[base + 2 * p, d:d + 1, :] = even[p:p + 1]
                pts[base + 2 * p + 1, d:d + 1, :] = odd[p:p + 1]
        return carry

    lax.fori_loop(0, n_sub, unpack, 0)
    vals[slots] = jnp.zeros((64, 64), jnp.bfloat16)
    pts[slots] = jnp.zeros((8, LANES), jnp.float32)

    def one_leaf(i, carry):
        cols = own_pts[i].T
        target = [jnp.broadcast_to(cols[:64, d:d + 1], (64, LANES)) for d in range(3)]
        values, highs, lows = [], [], []
        for p in range(4):
            a, b = idx[2 * p, i], idx[2 * p + 1, i]
            points = jnp.where(left8, pts[a], pts[b])
            values += [vals[a], vals[b]]
            dist = EPS_SQ
            for d in range(3):
                diff = target[d] - points[d:d + 1, :]
                dist = dist + diff * diff
            kern = lax.rsqrt(dist)
            high = kern.astype(jnp.bfloat16)
            highs.append(high)
            lows.append((kern - high.astype(jnp.float32)).astype(jnp.bfloat16))
        kernels = jnp.concatenate([jnp.concatenate(highs, axis=1), jnp.concatenate(lows, axis=1)], axis=0)
        full = jnp.dot(kernels, jnp.concatenate(values, axis=0), preferred_element_type=jnp.float32)
        top = full[:64]
        near = top[:, :32] + top[:, 32:] + full[64:, :32]
        out[i] = far[i] + INV_FOUR_PI * near.T
        return carry

    lax.fori_loop(0, leaves, one_leaf, 0, unroll=4)


def body(
    sources,
    coords,
    leaf_basis,
    transfer,
    send_list,
    near_list,
    near_count,
    far_list,
    coupling,
    group_transfer,
    group_coupling,
):
    n_sub = lax.axis_size("sub")
    n_grp = lax.axis_size("grp")
    leaves = sources.shape[2]
    par = leaves // CHILDREN
    cap = send_list.shape[1]
    slots = leaves + n_sub * cap
    near_entries = near_list.shape[0]
    f32 = jnp.float32

    x = jnp.transpose(sources, (2, 0, 1))
    own = jnp.concatenate([x, x], axis=2)
    y = jnp.transpose(coords, (2, 0, 1))
    own_pts = jnp.pad(jnp.concatenate([y, y], axis=2), ((0, 0), (0, 5), (0, 0)))
    basis = jnp.transpose(leaf_basis, (2, 0, 1)).reshape(leaves * 32, 64)
    trans = jnp.transpose(transfer, (2, 1, 0)).reshape(leaves * 32, 32)
    coup = jnp.transpose(coupling, (0, 2, 3, 1)).reshape(32 * 16 * par, 32)
    gt = jnp.transpose(group_transfer, (0, 2, 1)).reshape(32 * par, 32)
    gcoup = jnp.transpose(group_coupling, (0, 2, 3, 1)).reshape(32 * n_grp * n_grp, 32)
    live = jnp.arange(near_entries, dtype=jnp.int32)[:, None] < near_count[None, :]
    idx = jnp.pad(jnp.where(live, near_list, slots), ((0, 8 - near_entries), (0, 0)), constant_values=slots)

    vmem = pl.BlockSpec(memory_space=pltpu.VMEM)
    smem = pl.BlockSpec(memory_space=pltpu.SMEM)
    rows = 16 * cap + 3 * (cap // 2)
    dma = pltpu.SemaphoreType.DMA
    recv, far = pl.pallas_call(
        lambda *refs: exchange_kernel(n_grp, n_sub, par, cap, *refs),
        out_shape=(jax.ShapeDtypeStruct((n_sub, rows, LANES), f32),
                   jax.ShapeDtypeStruct((leaves * 32, 64), f32)),
        in_specs=[smem, smem] + [vmem] * 6 + [pl.BlockSpec(memory_space=pl.ANY)],
        out_specs=(vmem, vmem),
        scratch_shapes=[
            pltpu.VMEM((n_sub, rows, LANES), f32),
            pltpu.VMEM((n_sub * (par + 1), 8, LANES), f32),
            pltpu.VMEM((n_grp, 8, LANES), f32),
            pltpu.VMEM((n_sub * par, 32, LANES), f32),
            pltpu.VMEM((par, 32, LANES), f32),
            pltpu.VMEM((32 * 16 * par, 32), f32),
            dma((n_sub,)), dma((n_sub,)), dma((n_sub,)), dma((n_sub,)), dma((n_grp,)), dma((n_grp,)), dma,
        ],
        compiler_params=pltpu.CompilerParams(
            collective_id=0, has_side_effects=True, vmem_limit_bytes=48 * 2**20),
        name="exchange_far",
    )(send_list, far_list, own, own_pts, basis, trans, gt, gcoup, coup)

    out = pl.pallas_call(
        lambda *refs: near_kernel(n_sub, cap, slots, leaves, *refs),
        out_shape=jax.ShapeDtypeStruct((leaves, 32, 64), f32),
        in_specs=[smem] + [vmem] * 4,
        out_specs=vmem,
        scratch_shapes=[
            pltpu.VMEM((slots + 1, 64, 64), jnp.bfloat16),
            pltpu.VMEM((slots + 1, 8, LANES), f32),
        ],
        compiler_params=pltpu.CompilerParams(vmem_limit_bytes=48 * 2**20),
        name="near_field",
    )(idx, own, own_pts, recv, far.reshape(leaves, 32, 64))
    return jnp.transpose(out, (1, 2, 0))


def solution(mesh):
    whole = ("grp", "sub")
    return jax.shard_map(
        body,
        mesh=mesh,
        in_specs=(
            P(None, None, whole),
            P(None, None, whole),
            P(None, None, whole),
            P(None, None, whole),
            P(whole, None),
            P(None, whole),
            P(whole),
            P(None, whole),
            P(None, None, None, whole),
            P(None, None, whole),
            P(),
        ),
        out_specs=P(None, None, whole),
        check_vma=False,
    )
```

time: 134 us -> 113 us (0.84)
  local copies, waits for them, and re-layouts: 33.9 us -> 13.7 us
    unnamed x25 -> x22, local copies, waits for them, and re-layouts: 12.9 us -> 4.56 us
    transpose x4 -> x0, local copies, waits for them, and re-layouts: 7.22 us -> none  [the longest x1 6.85 us: body(): coupling.reshape(32, 4, 8, 16, par).transpose(4, 1, 0, 3, 2)]
    reshape x6 -> x0, local copies, waits for them, and re-layouts: 4.49 us -> none  [the longest x2 4.04 us: body(): coupling.reshape(32, 4, 8, 16, par).transpose(4, 1, 0, 3, 2)]
where the time goes in v1:
time: 113 us; the launch traced here: 112 us
  Pallas kernels  96.4 us (85%)
  local copies, waits for them, and re-layouts  13.7 us (12%)
  other arithmetic  2.16 us (2%)
    pallas_call x1, Pallas kernels, body(): pl.pallas_call(lambda *refs: exchange_kernel(n_grp, n_sub, par, cap, *ref...  64.4 us
    pallas_call x1, Pallas kernels, body(): pl.pallas_call(lambda *refs: near_kernel(n_sub, cap, slots, leaves, *refs...  32 us
    unnamed x22, local copies, waits for them, and re-layouts  4.56 us
    transpose x1, local copies, waits for them, and re-layouts, body(): basis = jnp.transpose(leaf_basis, (2, 0, 1)).reshape(leaves * 32, 64)  4.04 us
    transpose x1, local copies, waits for them, and re-layouts, body(): trans = jnp.transpose(transfer, (2, 1, 0)).reshape(leaves * 32, 32)  2.87 us
    transpose x1, local copies, waits for them, and re-layouts, body(): return jnp.transpose(out, (1, 2, 0))  2.26 us

profile of v1, /device:TPU:8, one launch (start us, length us, event | category | flops | bytes accessed | tf_op | source)
XLA Modules:
  0.0 112.4 jit_solution(15086148469225315448)
XLA Ops:
  0.0 3.1 %copy.12 = f32[32,64,128]{1,0,2:T(8,128)S(1)} copy(f32[32,64,128]{2,1,0:T(8,128)} %param.11) | data formatting | bytes 2097152 | tf_op args[0]
  3.1 0.0 copy-start.7
  3.1 1.9 %pad_maximum_fusion.refs_2_.refs_1_ = f32[128,32,128]{2,1,0:T(8,128)} fusion(f32[128,32,64]{2,1,0:T(8,128)S(1)} %bitcast.22), kind=kLoop, calls=%fused_computation | loop fusion | flops 524288 | bytes 3145728 | tf_op jit(solution)/shard_map/concatenate | solution.py:265
  5.0 0.0 copy-done.7
  5.0 0.0 copy-start.6
  5.0 0.1 copy.13
  5.2 0.2 select_maximum_fusion.refs_3_.refs_2_
  5.4 4.0 %copy.14 = f32[128,32,64]{2,1,0:T(8,128)} copy(f32[128,32,64]{0,2,1:T(8,128)} %bitcast.25) | data formatting | bytes 2097152 | tf_op jit(solution)/shard_map/transpose | solution.py:268
  9.4 0.0 copy-start.2
  9.4 0.0 copy-start.3
  9.4 0.0 copy-start.4
  9.4 0.0 copy-start.5
  9.4 0.0 copy-done.6
  9.5 2.9 %copy.15 = f32[128,32,32]{2,1,0:T(8,128)} copy(f32[128,32,32]{0,1,2:T(8,128)S(1)} %bitcast.27) | data formatting | bytes 1048576 | tf_op jit(solution)/shard_map/transpose | solution.py:269
  12.3 0.0 copy-done.2
  12.3 0.0 copy-done.3
  12.3 0.0 copy-done.4
  12.3 0.0 copy-done.5
  12.3 0.0 copy-start.8
  12.3 0.0 copy-start.9
  12.4 0.0 copy-start
  12.4 64.4 %exchange_far.1 = (f32[8,280,128]{2,1,0:T(8,128)S(1)}, f32[4096,64]{1,0:T(8,128)S(1)}) custom-call(s32[8,16]{1,0:T(8,128)S(1)} %copy-done.5, s32[16,16]{1,0:T(8,128)S(1)} %copy-done.4, f32[128,32,128]{2,1,0:T(8,128)} %pad_maximum_fusion.refs_2_.refs_1_, f32[128,8,128]{2,1,0:T(8,128)S(1)} %select_maximum_fusion.refs_3_.refs_2_, f32[4096,64]{1,0:T(8,128)} %bitcast.23, ...), custom_call_target="tpu_custom_call" | custom-call | tf_op jit(solution)/shard_map/exchange_far/pallas_call | solution.py:280
  76.8 0.0 copy-start.1
  76.8 1.3 %copy-done.1 = f32[4096,64]{1,0:T(8,128)} copy-done((f32[4096,64]{1,0:T(8,128)}, f32[4096,64]{1,0:T(8,128)S(1)}, u32[]{:S(2)}) %copy-start.1) | copy-done | bytes 1048600
  78.1 0.0 copy-done.8
  78.1 0.0 copy-done.9
  78.2 0.0 copy-done
  78.2 32.0 %near_field.1 = f32[128,32,64]{2,1,0:T(8,128)S(1)} custom-call(s32[8,128]{1,0:T(8,128)S(1)} %pad.8.refs_0_, f32[128,32,128]{2,1,0:T(8,128)S(1)} %copy-done, f32[128,8,128]{2,1,0:T(8,128)S(1)} %select_maximum_fusion.refs_3_.refs_2_, f32[8,280,128]{2,1,0:T(8,128)S(1)} %get-tuple-element.7.refs_3_, f32[128,32,64]{2,1,0:T(8,128)} %bitcast.18), custom_call_target="tpu_custom_call" | custom-call | tf_op jit(solution)/shard_map/near_field/pallas_call | solution.py:300
  110.1 2.3 %copy.16 = f32[32,64,128]{2,1,0:T(8,128)} copy(f32[32,64,128]{1,0,2:T(8,128)S(1)} %bitcast.17) | data formatting | bytes 2097152 | tf_op jit(solution)/shard_map/transpose | solution.py:312
  (2 shorter events, 0.0 us)
Async XLA Ops:
  3.1 2.0 %copy-start.7 = (f32[3,64,128]{2,1,0:T(8,128)S(1)}, f32[3,64,128]{2,1,0:T(8,128)}, u32[]{:S(2)}) copy-start(f32[3,64,128]{2,1,0:T(8,128)} %param.12) | copy-start | bytes 294916
  5.0 4.4 %copy-start.6 = (f32[32,32,128]{2,1,0:T(8,128)S(1)}, f32[32,32,128]{2,1,0:T(8,128)}, u32[]{:S(2)}) copy-start(f32[32,32,128]{2,1,0:T(8,128)} %param.14) | copy-start | bytes 1572868
  9.4 2.9 %copy-start.2 = (f32[32,32,16]{1,2,0:T(8,128)S(1)}, f32[32,32,16]{1,2,0:T(8,128)}, u32[]{:S(2)}) copy-start(f32[32,32,16]{1,2,0:T(8,128)} %param.20) | copy-start | bytes 196612
  9.4 2.9 %copy-start.3 = (f32[32,32,4,4]{1,3,2,0:T(4,128)S(1)}, f32[32,32,4,4]{1,3,2,0:T(4,128)}, u32[]{:S(2)}) copy-start(f32[32,32,4,4]{1,3,2,0:T(4,128)} %param.21) | copy-start | bytes 196612
  9.4 2.9 %copy-start.4 = (s32[16,16]{1,0:T(8,128)S(1)}, s32[16,16]{1,0:T(8,128)}, u32[]{:S(2)}) copy-start(s32[16,16]{1,0:T(8,128)} %refs_1_.1) | copy-start | bytes 3076
  9.4 2.9 %copy-start.5 = (s32[8,16]{1,0:T(8,128)S(1)}, s32[8,16]{1,0:T(8,128)}, u32[]{:S(2)}) copy-start(s32[8,16]{1,0:T(8,128)} %refs_0_.1) | copy-start | bytes 1540
  12.3 65.8 %copy-start.8 = (s32[7,128]{1,0:T(8,128)S(1)}, s32[7,128]{1,0:T(8,128)}, u32[]{:S(2)}) copy-start(s32[7,128]{1,0:T(8,128)} %param.16) | copy-start | bytes 10756
  12.3 65.8 %copy-start.9 = (s32[128]{0:T(128)S(1)}, s32[128]{0:T(128)}, u32[]{:S(2)}) copy-start(s32[128]{0:T(128)} %param.17) | copy-start | bytes 1540
  12.4 65.8 %copy-start = (f32[128,32,128]{2,1,0:T(8,128)S(1)}, f32[128,32,128]{2,1,0:T(8,128)}, u32[]{:S(2)}) copy-start(f32[128,32,128]{2,1,0:T(8,128)} %pad_maximum_fusion.refs_2_.refs_1_) | copy-start | bytes 6291460
  76.8 1.3 %copy-start.1 = (f32[4096,64]{1,0:T(8,128)}, f32[4096,64]{1,0:T(8,128)S(1)}, u32[]{:S(2)}) copy-start(f32[4096,64]{1,0:T(8,128)S(1)} %get-tuple-element.8) | copy-start | bytes 3145732

commit v2 on v1

--- a/solution.py
+++ b/solution.py
@@ -74,8 +74,8 @@
     def lift(c, carry):
         first = pl.multiple_of(c * CHILDREN, CHILDREN)
         rows = pl.ds(pl.multiple_of(c * 256, 256), 256)
-        vals = own[pl.ds(first, CHILDREN)].reshape(256, LANES)[:, :64]
-        skel = jnp.where(same, mm(basis[rows, :], vals, ((1,), (1,))), 0.0)
+        vals = jnp.concatenate([own[first + i] for i in range(CHILDREN)], axis=1)
+        skel = jnp.where(same, mm(basis[rows, :], vals), 0.0)
         up = mm(trans[rows, :], skel, ((0,), (0,)))
         y = up[:, :LANES] + up[:, LANES:]
         y = y + pltpu.roll(y, 64, 1)
@@ -96,7 +96,6 @@
     for o in range(1, n_sub):
         skel_copy(o).start()
 
-    left = lax.broadcasted_iota(jnp.int32, (16, LANES), 1) < 64
     left8 = lax.broadcasted_iota(jnp.int32, (8, LANES), 1) < 64
 
     def pack(peer, carry):
@@ -104,7 +103,7 @@
         for s in range(cap):
             leaf = send_list[peer, s]
             block = own[leaf]
-            send[peer, 16 * s:16 * s + 16, :] = jnp.where(left, block[:16], block[16:])
+            send[peer, 16 * s:16 * s + 16, :] = jnp.concatenate([block[16 * a:16 * a + 16] for a in range(4)], axis=1)
             tops.append(own_pts[leaf])
         for p in range(cap // 2):
             both = jnp.where(left8, tops[2 * p], tops[2 * p + 1])
@@ -177,63 +176,87 @@
         value_copy(o).wait()
 
 
-def near_kernel(n_sub, cap, slots, leaves, idx, own, own_pts, recv, far, out, vals, pts):
+def thirds(x):
+    terms = []
+    for _ in range(3):
+        term = x.astype(jnp.bfloat16).astype(jnp.float32)
+        terms.append(term)
+        x = x - term
+    return terms
+
+
+def near_kernel(n_sub, cap, slots, leaves, idx, own, own_pts, recv, far, out, vals, source, target):
     left8 = lax.broadcasted_iota(jnp.int32, (8, LANES), 1) < 64
-    left16 = lax.broadcasted_iota(jnp.int32, (16, LANES), 1) < 64
-
-    def put(slot, block):
+    left48 = lax.broadcasted_iota(jnp.int32, (48, LANES), 1) < 64
+    first16 = lax.broadcasted_iota(jnp.int32, (16, LANES), 1) < 32
+    first64 = lax.broadcasted_iota(jnp.int32, (64, 64), 1) < 32
+    row = lax.broadcasted_iota(jnp.int32, (8, LANES), 0)
+
+    def point_rows(tile):
+        centred = jnp.where(row < 3, tile - 1.0, 0.0)
+        return centred, jnp.sum(centred * centred, axis=0, keepdims=True)
+
+    def put_source(slot, tile):
+        y, norm = point_rows(tile)
+        u = thirds(jnp.where(row < 3, y, jnp.where(row == 3, norm, jnp.where(row == 4, 1.0, 0.0))))
+        rows = jnp.concatenate([u[0], u[1], u[0], u[1], u[2], u[0]], axis=0)
+        source[slot] = rows.astype(jnp.bfloat16)
+
+    def put_target(slot, tile):
+        x, norm = point_rows(tile)
+        w = thirds(jnp.where(row < 3, -2.0 * x, jnp.where(row == 3, 1.0, jnp.where(row == 4, norm + EPS_SQ, 0.0))))
+        rows = jnp.concatenate([w[0], w[0], w[1], w[1], w[0], w[2]], axis=0)
+        target[slot] = rows.T[:64].astype(jnp.bfloat16)
+
+    def keep(l, carry):
+        block = own[l]
         high = block.astype(jnp.bfloat16).astype(jnp.float32)
-        both = jnp.concatenate([high, block - high], axis=0)
-        vals[slot] = both.T[:64].astype(jnp.bfloat16)
-
-    def keep(l, carry):
-        put(l, own[l])
-        pts[l] = own_pts[l]
-        return carry
-
-    lax.fori_loop(0, leaves, keep, 0, unroll=8)
+        vals[l] = jnp.concatenate([high, block - high], axis=1).astype(jnp.bfloat16)
+        tile = own_pts[l]
+        put_source(l, tile)
+        put_target(l, tile)
+        return carry
+
+    lax.fori_loop(0, leaves, keep, 0, unroll=4)
 
     def unpack(peer, carry):
         base = leaves + peer * cap
         for s in range(cap):
             d = recv[peer, 16 * s:16 * s + 16, :]
-            turned = pltpu.roll(d, 64, 1)
-            put(base + s, jnp.concatenate([jnp.where(left16, d, turned), jnp.where(left16, turned, d)], axis=0))
+            high = d.astype(jnp.bfloat16).astype(jnp.float32)
+            low = d - high
+            rows = []
+            for a in range(4):
+                h = pltpu.roll(high, LANES - 32 * a, 1) if a else high
+                l = pltpu.roll(low, (LANES + 32 - 32 * a) % LANES, 1) if a != 1 else low
+                rows.append(jnp.where(first16, h, l))
+            vals[base + s] = jnp.concatenate(rows, axis=0)[:, :64].astype(jnp.bfloat16)
+        tiles = []
         for d in range(3):
             start = 16 * cap + (cap // 2) * d
             tile = recv[peer, start:start + cap // 2, :]
             turned = pltpu.roll(tile, 64, 1)
-            even, odd = jnp.where(left8, tile, turned), jnp.where(left8, turned, tile)
-            for p in range(cap // 2):
-                pts[base + 2 * p, d:d + 1, :] = even[p:p + 1]
-                pts[base + 2 * p + 1, d:d + 1, :] = odd[p:p + 1]
+            tiles.append((jnp.where(left8, tile, turned), jnp.where(left8, turned, tile)))
+        for s in range(cap):
+            parts = [jnp.broadcast_to(t[s % 2][s // 2:s // 2 + 1], (8, LANES)) for t in tiles]
+            put_source(base + s, jnp.where(row == 0, parts[0], jnp.where(row == 1, parts[1], parts[2])))
         return carry
 
     lax.fori_loop(0, n_sub, unpack, 0)
     vals[slots] = jnp.zeros((64, 64), jnp.bfloat16)
-    pts[slots] = jnp.zeros((8, LANES), jnp.float32)
+    put_source(slots, jnp.zeros((8, LANES), jnp.float32))
 
     def one_leaf(i, carry):
-        cols = own_pts[i].T
-        target = [jnp.broadcast_to(cols[:64, d:d + 1], (64, LANES)) for d in range(3)]
-        values, highs, lows = [], [], []
-        for p in range(4):
-            a, b = idx[2 * p, i], idx[2 * p + 1, i]
-            points = jnp.where(left8, pts[a], pts[b])
-            values += [vals[a], vals[b]]
-            dist = EPS_SQ
-            for d in range(3):
-                diff = target[d] - points[d:d + 1, :]
-                dist = dist + diff * diff
-            kern = lax.rsqrt(dist)
-            high = kern.astype(jnp.bfloat16)
-            highs.append(high)
-            lows.append((kern - high.astype(jnp.float32)).astype(jnp.bfloat16))
-        kernels = jnp.concatenate([jnp.concatenate(highs, axis=1), jnp.concatenate(lows, axis=1)], axis=0)
-        full = jnp.dot(kernels, jnp.concatenate(values, axis=0), preferred_element_type=jnp.float32)
-        top = full[:64]
-        near = top[:, :32] + top[:, 32:] + full[64:, :32]
-        out[i] = far[i] + INV_FOUR_PI * near.T
+        entries = [idx[e, i] for e in range(8)]
+        points = [jnp.where(left48, source[entries[2 * p]], source[entries[2 * p + 1]]) for p in range(4)]
+        dist = jnp.dot(target[i], jnp.concatenate(points, axis=1), preferred_element_type=jnp.float32)
+        kern = lax.rsqrt(dist)
+        high = kern.astype(jnp.bfloat16)
+        low = (kern - high.astype(jnp.float32)).astype(jnp.bfloat16)
+        values = jnp.concatenate([vals[e] for e in entries], axis=0)
+        full = jnp.dot(jnp.concatenate([high, low], axis=0), values, preferred_element_type=jnp.float32)
+        near = (full[:64] + jnp.where(first64, full[64:], 0.0)).T
+        out[i] = far[i] + INV_FOUR_PI * (near[:32] + near[32:])
         return carry
 
     lax.fori_loop(0, leaves, one_leaf, 0, unroll=4)
@@ -261,8 +284,7 @@
     near_entries = near_list.shape[0]
     f32 = jnp.float32
 
-    x = jnp.transpose(sources, (2, 0, 1))
-    own = jnp.concatenate([x, x], axis=2)
+    own = jnp.transpose(sources, (2, 1, 0))
     y = jnp.transpose(coords, (2, 0, 1))
     own_pts = jnp.pad(jnp.concatenate([y, y], axis=2), ((0, 0), (0, 5), (0, 0)))
     basis = jnp.transpose(leaf_basis, (2, 0, 1)).reshape(leaves * 32, 64)
@@ -304,7 +326,8 @@
         out_specs=vmem,
         scratch_shapes=[
             pltpu.VMEM((slots + 1, 64, 64), jnp.bfloat16),
-            pltpu.VMEM((slots + 1, 8, LANES), f32),
+            pltpu.VMEM((slots + 1, 48, LANES), jnp.bfloat16),
+            pltpu.VMEM((leaves, 64, 48), jnp.bfloat16),
         ],
         compiler_params=pltpu.CompilerParams(vmem_limit_bytes=48 * 2**20),
         name="near_field",

time: 113 us -> 117 us (1.035)
  Pallas kernels: 96.4 us -> 103 us
  other arithmetic: 2.16 us -> 0.21 us
    pallas_call x1, Pallas kernels: 32 us -> 37.3 us  [body(): pl.pallas_call(lambda *refs: near_kernel(n_sub, cap, slots, leaves, *refs...]
    concatenate x1 -> x0, other arithmetic: 1.95 us -> none  [body(): own = jnp.concatenate([x, x], axis=2)]
    transpose x1, local copies, waits for them, and re-layouts: 4.04 us -> 2.81 us  [body(): basis = jnp.transpose(leaf_basis, (2, 0, 1)).reshape(leaves * 32, 64)]
    unnamed x22 -> x20, local copies, waits for them, and re-layouts: 4.56 us -> 5.69 us
where the time goes in v2:
time: 117 us
  Pallas kernels  103 us (88%)
  local copies, waits for them, and re-layouts  13.7 us (12%)
    pallas_call x1, Pallas kernels, body(): pl.pallas_call(lambda *refs: exchange_kernel(n_grp, n_sub, par, cap, *ref...  65.5 us
    pallas_call x1, Pallas kernels, body(): pl.pallas_call(lambda *refs: near_kernel(n_sub, cap, slots, leaves, *refs...  37.3 us
    unnamed x20, local copies, waits for them, and re-layouts  5.69 us
    transpose x1, local copies, waits for them, and re-layouts, body(): trans = jnp.transpose(transfer, (2, 1, 0)).reshape(leaves * 32, 32)  2.88 us
    transpose x1, local copies, waits for them, and re-layouts, body(): basis = jnp.transpose(leaf_basis, (2, 0, 1)).reshape(leaves * 32, 64)  2.81 us

profile of v2, /device:TPU:8, one launch (start us, length us, event | category | flops | bytes accessed | tf_op | source)
XLA Modules:
  0.0 116.8 jit_solution(10634103045506829956)
XLA Ops:
  0.0 0.0 copy-start.6
  0.0 0.0 copy-start.4
  0.0 5.5 %copy.12 = f32[32,64,128]{0,1,2:T(8,128)} copy(f32[32,64,128]{2,1,0:T(8,128)} %param.11) | data formatting | bytes 2097152 | tf_op args[0]
  5.5 0.0 copy-done.6
  5.5 0.0 copy-start.5
  5.5 0.1 copy.13
  5.7 0.2 select_maximum_fusion.refs_3_.refs_2_
  5.9 0.0 copy-done.4
  5.9 2.8 %copy.14 = f32[128,32,64]{2,1,0:T(8,128)} copy(f32[128,32,64]{0,2,1:T(8,128)S(1)} %bitcast.26) | data formatting | bytes 2097152 | tf_op jit(solution)/shard_map/transpose | solution.py:290
  8.7 0.0 copy-start
  8.7 0.0 copy-start.1
  8.7 0.0 copy-start.2
  8.7 0.0 copy-start.3
  8.7 0.0 copy-done.5
  8.7 2.9 %copy.15 = f32[128,32,32]{2,1,0:T(8,128)} copy(f32[128,32,32]{0,1,2:T(8,128)S(1)} %bitcast.28) | data formatting | bytes 1048576 | tf_op jit(solution)/shard_map/transpose | solution.py:291
  11.6 0.0 copy-done
  11.6 0.0 copy-done.1
  11.6 0.0 copy-done.2
  11.6 0.0 copy-done.3
  11.6 0.0 copy-start.7
  11.6 0.0 copy-start.8
  11.6 65.5 %exchange_far.1 = (f32[8,280,128]{2,1,0:T(8,128)S(1)}, f32[4096,64]{1,0:T(8,128)S(1)}) custom-call(s32[8,16]{1,0:T(8,128)S(1)} %copy-done.3, s32[16,16]{1,0:T(8,128)S(1)} %copy-done.2, f32[128,64,32]{2,1,0:T(8,128)} %bitcast.21, f32[128,8,128]{2,1,0:T(8,128)S(1)} %select_maximum_fusion.refs_3_.refs_2_, f32[4096,64]{1,0:T(8,128)} %bitcast.24, ...), custom_call_target="tpu_custom_call" | custom-call | tf_op jit(solution)/shard_map/exchange_far/pallas_call | solution.py:302
  77.2 0.0 copy-done.7
  77.2 0.0 copy-done.8
  77.2 37.3 %near_field.1 = f32[128,32,64]{2,1,0:T(8,128)S(1)} custom-call(s32[8,128]{1,0:T(8,128)S(1)} %pad.8.refs_0_, f32[128,64,32]{2,1,0:T(8,128)} %bitcast.22, f32[128,8,128]{2,1,0:T(8,128)S(1)} %select_maximum_fusion.refs_3_.refs_2_, f32[8,280,128]{2,1,0:T(8,128)S(1)} %get-tuple-element.7.refs_3_, f32[128,32,64]{2,1,0:T(8,128)S(1)} %bitcast.18), custom_call_target="tpu_custom_call" | custom-call | tf_op jit(solution)/shard_map/near_field/pallas_call | solution.py:322
  114.5 2.3 %copy.16 = f32[32,64,128]{2,1,0:T(8,128)} copy(f32[32,64,128]{1,0,2:T(8,128)S(1)} %bitcast.17) | data formatting | bytes 2097152 | tf_op jit(solution)/shard_map/transpose | solution.py:335
  (2 shorter events, 0.0 us)
Async XLA Ops:
  0.0 5.5 %copy-start.6 = (f32[3,64,128]{2,1,0:T(8,128)S(1)}, f32[3,64,128]{2,1,0:T(8,128)}, u32[]{:S(2)}) copy-start(f32[3,64,128]{2,1,0:T(8,128)} %param.12) | copy-start | bytes 294916
  0.0 5.9 %copy-start.4 = (f32[32,64,128]{2,1,0:T(8,128)S(1)}, f32[32,64,128]{2,1,0:T(8,128)}, u32[]{:S(2)}) copy-start(f32[32,64,128]{2,1,0:T(8,128)} %param.13) | copy-start | bytes 3145732
  5.5 3.2 %copy-start.5 = (f32[32,32,128]{2,1,0:T(8,128)S(1)}, f32[32,32,128]{2,1,0:T(8,128)}, u32[]{:S(2)}) copy-start(f32[32,32,128]{2,1,0:T(8,128)} %param.14) | copy-start | bytes 1572868
  8.7 2.9 %copy-start = (f32[32,32,16]{1,2,0:T(8,128)S(1)}, f32[32,32,16]{1,2,0:T(8,128)}, u32[]{:S(2)}) copy-start(f32[32,32,16]{1,2,0:T(8,128)} %param.20) | copy-start | bytes 196612
  8.7 2.9 %copy-start.1 = (f32[32,32,4,4]{1,3,2,0:T(4,128)S(1)}, f32[32,32,4,4]{1,3,2,0:T(4,128)}, u32[]{:S(2)}) copy-start(f32[32,32,4,4]{1,3,2,0:T(4,128)} %param.21) | copy-start | bytes 196612
  8.7 2.9 %copy-start.2 = (s32[16,16]{1,0:T(8,128)S(1)}, s32[16,16]{1,0:T(8,128)}, u32[]{:S(2)}) copy-start(s32[16,16]{1,0:T(8,128)} %refs_1_.1) | copy-start | bytes 3076
  8.7 2.9 %copy-start.3 = (s32[8,16]{1,0:T(8,128)S(1)}, s32[8,16]{1,0:T(8,128)}, u32[]{:S(2)}) copy-start(s32[8,16]{1,0:T(8,128)} %refs_0_.1) | copy-start | bytes 1540
  11.6 65.6 %copy-start.7 = (s32[7,128]{1,0:T(8,128)S(1)}, s32[7,128]{1,0:T(8,128)}, u32[]{:S(2)}) copy-start(s32[7,128]{1,0:T(8,128)} %param.16) | copy-start | bytes 10756
  11.6 65.6 %copy-start.8 = (s32[128]{0:T(128)S(1)}, s32[128]{0:T(128)}, u32[]{:S(2)}) copy-start(s32[128]{0:T(128)} %param.17) | copy-start | bytes 1540

commit v3 on v1

v3 whole, which is shorter than its diff:
```python
import math

import jax
import jax.numpy as jnp
from jax import lax
from jax.experimental import pallas as pl
from jax.experimental.pallas import tpu as pltpu
from jax.sharding import PartitionSpec as P

INV_FOUR_PI = 1.0 / (4.0 * math.pi)
EPS_SQ = 0.01
MESH = pl.DeviceIdType.MESH
LANES = 128
CHILDREN = 8
TOGETHER = 4


def halves(x):
    high = x.astype(jnp.bfloat16)
    return high, (x - high.astype(jnp.float32)).astype(jnp.bfloat16)


def mm(a, b, dims=((1,), (0,))):
    def dot(x, y):
        return lax.dot_general(x, y, (dims, ((), ())), preferred_element_type=jnp.float32)
    a0, a1 = halves(a)
    b0, b1 = halves(b)
    return dot(a0, b0) + (dot(a0, b1) + dot(a1, b0))


def lane_block(rows):
    return lax.broadcasted_iota(jnp.int32, (rows, LANES), 1) // 32


def pick_blocks(parts):
    blk = lane_block(parts[0].shape[0])
    out = parts[3]
    for a in (2, 1, 0):
        out = jnp.where(blk == a, parts[a], out)
    return out


def spread_lanes(y):
    y = jnp.where(lane_block(y.shape[0]) == 0, y, 0.0)
    y = y + pltpu.roll(y, 32, 1)
    return y + pltpu.roll(y, 64, 1)


def loose(block):
    return jnp.concatenate([block] + [pltpu.roll(block, LANES - 32 * a, 1) for a in range(1, 4)], axis=0)


def dense(y):
    return pick_blocks([y[8 * a:8 * a + 8] for a in range(4)])


def thirds(x):
    terms = []
    for _ in range(3):
        term = x.astype(jnp.bfloat16).astype(jnp.float32)
        terms.append(term)
        x = x - term
    return terms


def point_rows(tile):
    row = lax.broadcasted_iota(jnp.int32, (8, LANES), 0)
    centred = jnp.where(row < 3, tile - 1.0, 0.0)
    return row, centred, jnp.sum(centred * centred, axis=0, keepdims=True)


def source_rows(tile):
    row, y, norm = point_rows(tile)
    u = thirds(jnp.where(row < 3, y, jnp.where(row == 3, norm, jnp.where(row == 4, 1.0, 0.0))))
    return jnp.concatenate([u[0], u[1], u[0], u[1], u[2], u[0]], axis=0).astype(jnp.bfloat16)


def target_columns(tile):
    row, x, norm = point_rows(tile)
    w = thirds(jnp.where(row < 3, -2.0 * x, jnp.where(row == 3, 1.0, jnp.where(row == 4, norm + EPS_SQ, 0.0))))
    rows = jnp.concatenate([w[0], w[0], w[1], w[1], w[0], w[2]], axis=0)
    return rows.T[:64].astype(jnp.bfloat16)


def unpack(cap, base, got, vals, source):
    first16 = lax.broadcasted_iota(jnp.int32, (16, LANES), 1) < 32
    left8 = lax.broadcasted_iota(jnp.int32, (8, LANES), 1) < 64
    row = lax.broadcasted_iota(jnp.int32, (8, LANES), 0)
    for s in range(cap):
        d = got[16 * s:16 * s + 16, :]
        high = d.astype(jnp.bfloat16).astype(jnp.float32)
        low = d - high
        rows = []
        for a in range(4):
            h = pltpu.roll(high, LANES - 32 * a, 1) if a else high
            l = pltpu.roll(low, (LANES + 32 - 32 * a) % LANES, 1) if a != 1 else low
            rows.append(jnp.where(first16, h, l))
        vals[base + s] = jnp.concatenate(rows, axis=0)[:, :64].astype(jnp.bfloat16)
    tiles = []
    for d in range(3):
        start = 16 * cap + (cap // 2) * d
        tile = got[start:start + cap // 2, :]
        turned = pltpu.roll(tile, 64, 1)
        tiles.append((jnp.where(left8, tile, turned), jnp.where(left8, turned, tile)))
    for s in range(cap):
        parts = [jnp.broadcast_to(t[s % 2][s // 2:s // 2 + 1], (8, LANES)) for t in tiles]
        source[base + s] = source_rows(jnp.where(row == 0, parts[0], jnp.where(row == 1, parts[1], parts[2])))


def exchange_kernel(n_grp, n_sub, par, cap, slots,
                    send_list, far_list, own, own_pts, basis, trans, gt, gcoup, coup_hbm,
                    vals, source, target, far,
                    send, recv, ps_all, gs_all, loose_all, field, coup, send_sem, recv_sem, ps_send, ps_recv, gs_send,
                    gs_recv, coup_sem):
    me = lax.axis_index("sub")
    grp = lax.axis_index("grp")
    barrier = pltpu.get_barrier_semaphore()
    for o in range(1, n_sub):
        pl.semaphore_signal(barrier, inc=1, device_id={"sub": lax.rem(me + o, n_sub)}, device_id_type=MESH)
    for o in range(1, n_grp):
        pl.semaphore_signal(barrier, inc=1, device_id={"grp": lax.rem(grp + o, n_grp)}, device_id_type=MESH)

    coup_copy = pltpu.make_async_copy(coup_hbm, coup, coup_sem)
    coup_copy.start()
    left8 = lax.broadcasted_iota(jnp.int32, (8, LANES), 1) < 64

    def pack(peer, carry):
        tops = []
        for s in range(cap):
            leaf = send_list[peer, s]
            block = own[leaf]
            send[peer, 16 * s:16 * s + 16, :] = jnp.concatenate([block[16 * a:16 * a + 16] for a in range(4)], axis=1)
            tops.append(own_pts[leaf])
        for p in range(cap // 2):
            both = jnp.where(left8, tops[2 * p], tops[2 * p + 1])
            for d in range(3):
                row = 16 * cap + (cap // 2) * d + p
                send[peer, row:row + 1, :] = both[d:d + 1]
        return carry

    lax.fori_loop(0, n_sub, pack, 0)
    def value_copy(o):
        peer = lax.rem(me + o, n_sub)
        return pltpu.make_async_remote_copy(
            src_ref=send.at[peer], dst_ref=recv.at[me], send_sem=send_sem.at[o], recv_sem=recv_sem.at[o],
            device_id={"sub": peer}, device_id_type=MESH)

    pl.semaphore_wait(barrier, n_sub - 1 + n_grp - 1)
    early = n_sub // 2
    for o in range(1, early):
        value_copy(o).start()

    same = (lax.broadcasted_iota(jnp.int32, (256, 256), 0) // 32
            == lax.broadcasted_iota(jnp.int32, (256, 256), 1) // 32)

    def lift(c, carry):
        first = pl.multiple_of(c * CHILDREN, CHILDREN)
        rows = pl.ds(pl.multiple_of(c * 256, 256), 256)
        vals = jnp.concatenate([own[first + i] for i in range(CHILDREN)], axis=1)
        skel = jnp.where(same, mm(basis[rows, :], vals), 0.0)
        up = mm(trans[rows, :], skel, ((0,), (0,)))
        y = up[:, :LANES] + up[:, LANES:]
        y = y + pltpu.roll(y, 64, 1)
        y = y + pltpu.roll(y, 32, 1)
        ps_all[me * (par + 1) + c] = dense(y)
        return carry + mm(gt[pl.ds(c, 32, stride=par), :], y)

    part = lax.fori_loop(0, par, lift, jnp.zeros((32, LANES), jnp.float32))
    ps_all[me * (par + 1) + par] = dense(part)

    partner = me + 1 - 2 * lax.rem(me, 2)

    def skel_copy(whose, to, k):
        part = ps_all.at[pl.ds(whose * (par + 1), par + 1)]
        return pltpu.make_async_remote_copy(
            src_ref=part, dst_ref=part, send_sem=ps_send.at[k], recv_sem=ps_recv.at[k],
            device_id={"sub": to}, device_id_type=MESH)

    def direct(o):
        return skel_copy(me, lax.rem(me + o, n_sub), o)

    def forward(o):
        return skel_copy(lax.rem(me + n_sub - o, n_sub), partner, o + 1)

    for o in range(2, n_sub, 2):
        direct(o).start()
    skel_copy(me, partner, 1).start()
    for o in range(early, n_sub):
        value_copy(o).start()

    def keep(l, carry):
        block = own[l]
        high = block.astype(jnp.bfloat16).astype(jnp.float32)
        vals[l] = jnp.concatenate([high, block - high], axis=1).astype(jnp.bfloat16)
        source[l] = source_rows(own_pts[l])
        return carry

    def keep_target(l, carry):
        target[l] = target_columns(own_pts[l])
        return carry

    lax.fori_loop(0, par * CHILDREN, keep, 0, unroll=4)
    vals[slots] = jnp.zeros((64, 64), jnp.bfloat16)
    source[slots] = source_rows(jnp.zeros((8, LANES), jnp.float32))
    for o in range(2, n_sub, 2):
        direct(o).wait_recv()
        forward(o).start()
    lax.fori_loop(0, par * CHILDREN, keep_target, 0, unroll=4)
    unpack(cap, par * CHILDREN + me * cap, send.at[me], vals, source)
    for o in range(2, n_sub, 2):
        direct(o).wait_send()
        forward(o).wait()
    skel_copy(me, partner, 1).wait()

    total = ps_all[par]
    for m in range(1, n_sub):
        total = total + ps_all[m * (par + 1) + par]
    gs_all[grp] = total

    def group_copy(o):
        return pltpu.make_async_remote_copy(
            src_ref=gs_all.at[grp], dst_ref=gs_all.at[grp], send_sem=gs_send.at[o], recv_sem=gs_recv.at[o],
            device_id={"grp": lax.rem(grp + o, n_grp)}, device_id_type=MESH)

    for o in range(1, n_grp):
        group_copy(o).start()

    def loosen(m, carry):
        for c in range(par):
            loose_all[m * par + c] = loose(ps_all[m * (par + 1) + c])
        return carry

    lax.fori_loop(0, n_sub, loosen, 0)
    coup_copy.wait()

    def local(c, carry):
        partners = jnp.concatenate([loose_all[far_list[f, c]] for f in range(16)], axis=0)
        blocks = jnp.concatenate([coup[pl.ds(f * par + c, 32, stride=16 * par), :] for f in range(16)], axis=1)
        field[c] = spread_lanes(mm(blocks, partners))
        return carry

    lax.fori_loop(0, par, local, 0)
    for o in range(1, n_grp):
        group_copy(o).wait()
    inflow = jnp.zeros((32, LANES), jnp.float32)
    for h in range(n_grp):
        live = jnp.where(grp == h, 0.0, 1.0)
        block = gcoup[pl.ds(grp * n_grp + h, 32, stride=n_grp * n_grp), :]
        inflow = inflow + mm(block * live, loose(gs_all[h]))
    inflow = spread_lanes(inflow)

    def down(c, carry):
        rows = pl.ds(pl.multiple_of(c * 256, 256), 256)
        here = field[c] + mm(gt[pl.ds(c, 32, stride=par), :], inflow, ((0,), (0,)))
        leaf_field = mm(here.T, trans[rows, :], ((1,), (1,)))
        spread = jnp.where(same, jnp.concatenate([leaf_field, leaf_field], axis=0), 0.0)
        far[rows, :] = mm(spread, basis[rows, :])
        return carry

    lax.fori_loop(0, par, down, 0)

    def arrive(o, carry):
        value_copy(o).wait_recv()
        sender = lax.rem(me + n_sub - o, n_sub)
        unpack(cap, par * CHILDREN + sender * cap, recv.at[sender], vals, source)
        return carry

    lax.fori_loop(1, n_sub, arrive, 0)
    for o in range(1, n_sub):
        value_copy(o).wait_send()


def near_kernel(leaves, idx, vals, source, target, far, out):
    left48 = lax.broadcasted_iota(jnp.int32, (48, LANES), 1) < 64
    first64 = lax.broadcasted_iota(jnp.int32, (64, 64), 1) < 32

    def some_leaves(step, carry):
        ids = [step * TOGETHER + n for n in range(TOGETHER)]
        entries = [[idx[e, i] for e in range(8)] for i in ids]
        dists = []
        for i, ent in zip(ids, entries):
            points = [jnp.where(left48, source[ent[2 * p]], source[ent[2 * p + 1]]) for p in range(4)]
            dists.append(jnp.dot(target[i], jnp.concatenate(points, axis=1), preferred_element_type=jnp.float32))
        sides = []
        for dist in dists:
            kern = lax.rsqrt(dist)
            high = kern.astype(jnp.bfloat16)
            low = (kern - high.astype(jnp.float32)).astype(jnp.bfloat16)
            sides.append(jnp.concatenate([high, low], axis=0))
        fulls = []
        for ent, side in zip(entries, sides):
            values = jnp.concatenate([vals[e] for e in ent], axis=0)
            fulls.append(jnp.dot(side, values, preferred_element_type=jnp.float32))
        nears = [(full[:64] + jnp.where(first64, full[64:], 0.0)).T for full in fulls]
        for i, near in zip(ids, nears):
            out[i] = far[i] + INV_FOUR_PI * (near[:32] + near[32:])
        return carry

    lax.fori_loop(0, leaves // TOGETHER, some_leaves, 0)


def body(
    sources,
    coords,
    leaf_basis,
    transfer,
    send_list,
    near_list,
    near_count,
    far_list,
    coupling,
    group_transfer,
    group_coupling,
):
    n_sub = lax.axis_size("sub")
    n_grp = lax.axis_size("grp")
    leaves = sources.shape[2]
    par = leaves // CHILDREN
    cap = send_list.shape[1]
    slots = leaves + n_sub * cap
    near_entries = near_list.shape[0]
    f32 = jnp.float32

    own = jnp.transpose(sources, (2, 1, 0))
    y = jnp.transpose(coords, (2, 0, 1))
    own_pts = jnp.pad(jnp.concatenate([y, y], axis=2), ((0, 0), (0, 5), (0, 0)))
    basis = jnp.transpose(leaf_basis, (2, 0, 1)).reshape(leaves * 32, 64)
    trans = jnp.transpose(transfer, (2, 1, 0)).reshape(leaves * 32, 32)
    coup = jnp.transpose(coupling, (0, 2, 3, 1)).reshape(32 * 16 * par, 32)
    gt = jnp.transpose(group_transfer, (0, 2, 1)).reshape(32 * par, 32)
    gcoup = jnp.transpose(group_coupling, (0, 2, 3, 1)).reshape(32 * n_grp * n_grp, 32)
    live = jnp.arange(near_entries, dtype=jnp.int32)[:, None] < near_count[None, :]
    idx = jnp.pad(jnp.where(live, near_list, slots), ((0, 8 - near_entries), (0, 0)), constant_values=slots)

    vmem = pl.BlockSpec(memory_space=pltpu.VMEM)
    smem = pl.BlockSpec(memory_space=pltpu.SMEM)
    rows = 16 * cap + 3 * (cap // 2)
    dma = pltpu.SemaphoreType.DMA
    vals, source, target, far = pl.pallas_call(
        lambda *refs: exchange_kernel(n_grp, n_sub, par, cap, slots, *refs),
        out_shape=(jax.ShapeDtypeStruct((slots + 1, 64, 64), jnp.bfloat16),
                   jax.ShapeDtypeStruct((slots + 1, 48, LANES), jnp.bfloat16),
                   jax.ShapeDtypeStruct((leaves, 64, 48), jnp.bfloat16),
                   jax.ShapeDtypeStruct((leaves * 32, 64), f32)),
        in_specs=[smem, smem] + [vmem] * 6 + [pl.BlockSpec(memory_space=pl.ANY)],
        out_specs=(vmem,) * 4,
        scratch_shapes=[
            pltpu.VMEM((n_sub, rows, LANES), f32),
            pltpu.VMEM((n_sub, rows, LANES), f32),
            pltpu.VMEM((n_sub * (par + 1), 8, LANES), f32),
            pltpu.VMEM((n_grp, 8, LANES), f32),
            pltpu.VMEM((n_sub * par, 32, LANES), f32),
            pltpu.VMEM((par, 32, LANES), f32),
            pltpu.VMEM((32 * 16 * par, 32), f32),
            dma((n_sub,)), dma((n_sub,)), dma((n_sub,)), dma((n_sub,)), dma((n_grp,)), dma((n_grp,)), dma,
        ],
        compiler_params=pltpu.CompilerParams(
            collective_id=0, has_side_effects=True, vmem_limit_bytes=40 * 2**20),
        name="exchange_far",
    )(send_list, far_list, own, own_pts, basis, trans, gt, gcoup, coup)

    out = pl.pallas_call(
        lambda *refs: near_kernel(leaves, *refs),
        out_shape=jax.ShapeDtypeStruct((leaves, 32, 64), f32),
        in_specs=[smem] + [vmem] * 4,
        out_specs=vmem,
        compiler_params=pltpu.CompilerParams(vmem_limit_bytes=32 * 2**20),
        name="near_field",
    )(idx, vals, source, target, far.reshape(leaves, 32, 64))
    return jnp.transpose(out, (1, 2, 0))


def solution(mesh):
    whole = ("grp", "sub")
    return jax.shard_map(
        body,
        mesh=mesh,
        in_specs=(
            P(None, None, whole),
            P(None, None, whole),
            P(None, None, whole),
            P(None, None, whole),
            P(whole, None),
            P(None, whole),
            P(whole),
            P(None, whole),
            P(None, None, None, whole),
            P(None, None, whole),
            P(),
        ),
        out_specs=P(None, None, whole),
        check_vma=False,
    )
```

time: 113 us -> 104 us (0.920)
  the two profiles are of different devices: /device:TPU:8 before, /device:TPU:26 now
where the time goes in v3:
time: 104 us
  Pallas kernels  86.9 us (84%)
  local copies, waits for them, and re-layouts  16.5 us (16%)
    pallas_call x1, Pallas kernels, body(): pl.pallas_call(lambda *refs: exchange_kernel(n_grp, n_sub, par, cap, slot...  70.7 us
    pallas_call x1, Pallas kernels, body(): pl.pallas_call(lambda *refs: near_kernel(leaves, *refs), out_shape=jax.Sh...  16.3 us
    unnamed x24, local copies, waits for them, and re-layouts  9.46 us
    transpose x1, local copies, waits for them, and re-layouts, body(): basis = jnp.transpose(leaf_basis, (2, 0, 1)).reshape(leaves * 32, 64)  2.82 us
    transpose x1, local copies, waits for them, and re-layouts, body(): return jnp.transpose(out, (1, 2, 0))  2.26 us

profile of v3, /device:TPU:26, one launch (start us, length us, event | category | flops | bytes accessed | tf_op | source)
XLA Modules:
  0.0 103.8 jit_solution(12221691106713828174)
XLA Ops:
  0.0 0.0 copy-start.6
  0.0 5.5 %copy.12 = f32[32,64,128]{0,1,2:T(8,128)} copy(f32[32,64,128]{2,1,0:T(8,128)} %param.11) | data formatting | bytes 2097152 | tf_op args[0]
  5.5 0.0 copy-start.7
  5.5 0.0 copy-done.6
  5.5 2.8 %copy.14 = f32[128,32,64]{2,1,0:T(8,128)} copy(f32[128,32,64]{0,2,1:T(8,128)S(1)} %bitcast.25) | data formatting | bytes 2097152 | tf_op jit(solution)/shard_map/transpose | solution.py:327
  8.3 0.0 copy-start.8
  8.3 0.0 copy-start.2
  8.3 0.0 copy-start.3
  8.3 0.0 copy-start.4
  8.4 0.0 copy-start.5
  8.4 0.0 copy-done.7
  8.4 1.9 %copy.15 = f32[128,32,32]{2,1,0:T(8,128)S(1)} copy(f32[128,32,32]{0,1,2:T(8,128)S(1)} %bitcast.27) | data formatting | bytes 1048576 | tf_op jit(solution)/shard_map/transpose | solution.py:328
  10.3 0.0 copy-done.8
  10.3 0.1 copy.13
  10.4 0.2 select_maximum_fusion.refs_3_
  10.7 0.0 copy-done.2
  10.7 0.0 copy-done.3
  10.7 0.0 copy-done.4
  10.7 0.0 copy-done.5
  10.7 0.0 copy-start
  10.7 1.6 %copy-done = f32[128,32,64]{2,1,0:T(8,128)S(1)} copy-done((f32[128,32,64]{2,1,0:T(8,128)S(1)}, f32[128,32,64]{2,1,0:T(8,128)}, u32[]{:S(2)}) %copy-start) | copy-done | bytes 1048600
  12.3 0.0 copy-start.9
  12.3 0.0 copy-start.10
  12.3 70.7 %exchange_far.1 = (bf16[257,64,64]{2,1,0:T(8,128)(2,1)}, bf16[257,48,128]{2,1,0:T(8,128)(2,1)S(1)}, bf16[128,64,48]{2,1,0:T(8,128)(2,1)S(1)}, f32[4096,64]{1,0:T(8,128)S(1)}) custom-call(s32[8,16]{1,0:T(8,128)S(1)} %copy-done.5, s32[16,16]{1,0:T(8,128)S(1)} %copy-done.4, f32[128,64,32]{2,1,0:T(8,128)} %bitcast.23, ...), custom_call_target="tpu_custom_call" | custom-call | tf_op jit(solution)/shard_map/exchange_far/pallas_call | solution.py:339
  83.0 0.0 copy-done.9
  83.0 0.0 copy-done.10
  83.0 0.0 copy-start.1
  83.0 2.2 %copy-done.1 = bf16[257,64,64]{2,1,0:T(8,128)(2,1)S(1)} copy-done((bf16[257,64,64]{2,1,0:T(8,128)(2,1)S(1)}, bf16[257,64,64]{2,1,0:T(8,128)(2,1)}, u32[]{:S(2)}) %copy-start.1) | copy-done | bytes 2105368
  85.2 16.3 %near_field.1 = f32[128,32,64]{2,1,0:T(8,128)S(1)} custom-call(s32[8,128]{1,0:T(8,128)S(1)} %pad.8.refs_0_, bf16[257,64,64]{2,1,0:T(8,128)(2,1)S(1)} %copy-done.1, bf16[257,48,128]{2,1,0:T(8,128)(2,1)S(1)} %get-tuple-element.10.refs_2_, bf16[128,64,48]{2,1,0:T(8,128)(2,1)S(1)} %get-tuple-element.11.refs_3_, f32[128,32,64]{2,1,0:T(8,128)S(1)} %bitcast.20), custom_call_target="tpu_custom_call" | custom-call | tf_op jit(solution)/shard_map/near_field/pallas_call | solution.py:362
  101.5 2.3 %copy.16 = f32[32,64,128]{2,1,0:T(8,128)} copy(f32[32,64,128]{1,0,2:T(8,128)S(1)} %bitcast.19) | data formatting | bytes 2097152 | tf_op jit(solution)/shard_map/transpose | solution.py:370
  (2 shorter events, 0.0 us)
Async XLA Ops:
  0.0 5.5 %copy-start.6 = (f32[32,64,128]{2,1,0:T(8,128)S(1)}, f32[32,64,128]{2,1,0:T(8,128)}, u32[]{:S(2)}) copy-start(f32[32,64,128]{2,1,0:T(8,128)} %param.13) | copy-start | bytes 3145732
  5.5 2.9 %copy-start.7 = (f32[32,32,128]{2,1,0:T(8,128)S(1)}, f32[32,32,128]{2,1,0:T(8,128)}, u32[]{:S(2)}) copy-start(f32[32,32,128]{2,1,0:T(8,128)} %param.14) | copy-start | bytes 1572868
  8.3 1.9 %copy-start.8 = (f32[3,64,128]{2,1,0:T(8,128)S(1)}, f32[3,64,128]{2,1,0:T(8,128)}, u32[]{:S(2)}) copy-start(f32[3,64,128]{2,1,0:T(8,128)} %param.12) | copy-start | bytes 294916
  8.3 2.3 %copy-start.2 = (f32[32,32,16]{1,2,0:T(8,128)S(1)}, f32[32,32,16]{1,2,0:T(8,128)}, u32[]{:S(2)}) copy-start(f32[32,32,16]{1,2,0:T(8,128)} %param.20) | copy-start | bytes 196612
  8.3 2.3 %copy-start.3 = (f32[32,32,4,4]{1,3,2,0:T(4,128)S(1)}, f32[32,32,4,4]{1,3,2,0:T(4,128)}, u32[]{:S(2)}) copy-start(f32[32,32,4,4]{1,3,2,0:T(4,128)} %param.21) | copy-start | bytes 196612
  8.3 2.3 %copy-start.4 = (s32[16,16]{1,0:T(8,128)S(1)}, s32[16,16]{1,0:T(8,128)}, u32[]{:S(2)}) copy-start(s32[16,16]{1,0:T(8,128)} %refs_1_.1) | copy-start | bytes 3076
  8.4 2.3 %copy-start.5 = (s32[8,16]{1,0:T(8,128)S(1)}, s32[8,16]{1,0:T(8,128)}, u32[]{:S(2)}) copy-start(s32[8,16]{1,0:T(8,128)} %refs_0_.1) | copy-start | bytes 1540
  10.7 1.6 %copy-start = (f32[128,32,64]{2,1,0:T(8,128)S(1)}, f32[128,32,64]{2,1,0:T(8,128)}, u32[]{:S(2)}) copy-start(f32[128,32,64]{2,1,0:T(8,128)} %copy.14) | copy-start | bytes 3145732
  12.3 70.7 %copy-start.9 = (s32[7,128]{1,0:T(8,128)S(1)}, s32[7,128]{1,0:T(8,128)}, u32[]{:S(2)}) copy-start(s32[7,128]{1,0:T(8,128)} %param.16) | copy-start | bytes 10756
  12.3 70.7 %copy-start.10 = (s32[128]{0:T(128)S(1)}, s32[128]{0:T(128)}, u32[]{:S(2)}) copy-start(s32[128]{0:T(128)} %param.17) | copy-start | bytes 1540
  83.0 2.2 %copy-start.1 = (bf16[257,64,64]{2,1,0:T(8,128)(2,1)S(1)}, bf16[257,64,64]{2,1,0:T(8,128)(2,1)}, u32[]{:S(2)}) copy-start(bf16[257,64,64]{2,1,0:T(8,128)(2,1)} %get-tuple-element.9.refs_1_) | copy-start | bytes 6316036

commit v4 on v3

--- a/solution.py
+++ b/solution.py
@@ -82,20 +82,31 @@
     return rows.T[:64].astype(jnp.bfloat16)
 
 
+def value_rows(d):
+    first16 = lax.broadcasted_iota(jnp.int32, (16, LANES), 1) < 32
+    high = d.astype(jnp.bfloat16).astype(jnp.float32)
+    low = d - high
+    rows = []
+    for a in range(4):
+        h = pltpu.roll(high, LANES - 32 * a, 1) if a else high
+        l = pltpu.roll(low, (LANES + 32 - 32 * a) % LANES, 1) if a != 1 else low
+        rows.append(jnp.where(first16, h, l))
+    return jnp.concatenate(rows, axis=0)[:, :64].astype(jnp.bfloat16)
+
+
+def xor(i, k, size):
+    out, bit = 0, 1
+    while bit < size:
+        x, y = lax.rem(i // bit, 2), lax.rem(k // bit, 2)
+        out, bit = out + bit * (x + y - 2 * x * y), 2 * bit
+    return out
+
+
 def unpack(cap, base, got, vals, source):
-    first16 = lax.broadcasted_iota(jnp.int32, (16, LANES), 1) < 32
     left8 = lax.broadcasted_iota(jnp.int32, (8, LANES), 1) < 64
     row = lax.broadcasted_iota(jnp.int32, (8, LANES), 0)
     for s in range(cap):
-        d = got[16 * s:16 * s + 16, :]
-        high = d.astype(jnp.bfloat16).astype(jnp.float32)
-        low = d - high
-        rows = []
-        for a in range(4):
-            h = pltpu.roll(high, LANES - 32 * a, 1) if a else high
-            l = pltpu.roll(low, (LANES + 32 - 32 * a) % LANES, 1) if a != 1 else low
-            rows.append(jnp.where(first16, h, l))
-        vals[base + s] = jnp.concatenate(rows, axis=0)[:, :64].astype(jnp.bfloat16)
+        vals[base + s] = value_rows(got[16 * s:16 * s + 16, :])
     tiles = []
     for d in range(3):
         start = 16 * cap + (cap // 2) * d
@@ -108,28 +119,46 @@
 
 
 def exchange_kernel(n_grp, n_sub, par, cap, slots,
-                    send_list, far_list, own, own_pts, basis, trans, gt, gcoup, coup_hbm,
+                    send_list, far_list, src, own_pts, raw_basis, raw_trans, gt, gcoup, coup_hbm,
                     vals, source, target, far,
-                    send, recv, ps_all, gs_all, loose_all, field, coup, send_sem, recv_sem, ps_send, ps_recv, gs_send,
+                    flat, own, basis, trans, send, recv, ps_all, gs_all, loose_all, field, coup, send_sem, recv_sem, ps_send, ps_recv, gs_send,
                     gs_recv, coup_sem):
     me = lax.axis_index("sub")
     grp = lax.axis_index("grp")
     barrier = pltpu.get_barrier_semaphore()
-    for o in range(1, n_sub):
-        pl.semaphore_signal(barrier, inc=1, device_id={"sub": lax.rem(me + o, n_sub)}, device_id_type=MESH)
+    peers = [me] + [xor(me, k, n_sub) for k in range(1, n_sub)]
+    for k in range(1, n_sub):
+        pl.semaphore_signal(barrier, inc=1, device_id={"sub": peers[k]}, device_id_type=MESH)
     for o in range(1, n_grp):
         pl.semaphore_signal(barrier, inc=1, device_id={"grp": lax.rem(grp + o, n_grp)}, device_id_type=MESH)
 
     coup_copy = pltpu.make_async_copy(coup_hbm, coup, coup_sem)
     coup_copy.start()
+    leaves = par * CHILDREN
+
+    def turn_sources(q, carry):
+        cols = jnp.concatenate([src[pl.ds(16 * a + q, 32, stride=64), :] for a in range(4)], axis=0)
+        flat[pl.ds(q, leaves, stride=16), :] = cols.T
+        return carry
+
+    def turn_basis(k, carry):
+        basis[pl.ds(k, leaves, stride=32), :] = raw_basis[pl.ds(pl.multiple_of(64 * k, 64), 64), :].T
+        trans[pl.ds(k, leaves, stride=32), :] = raw_trans[pl.ds(k, 32, stride=32), :].T
+        return carry
+
+    def own_copy(l, carry):
+        own[l] = flat[pl.ds(pl.multiple_of(16 * l, 16), 16), :]
+        return carry
+
+    lax.fori_loop(0, 16, turn_sources, 0, unroll=2)
+    lax.fori_loop(0, leaves, own_copy, 0, unroll=16)
     left8 = lax.broadcasted_iota(jnp.int32, (8, LANES), 1) < 64
 
     def pack(peer, carry):
         tops = []
         for s in range(cap):
             leaf = send_list[peer, s]
-            block = own[leaf]
-            send[peer, 16 * s:16 * s + 16, :] = jnp.concatenate([block[16 * a:16 * a + 16] for a in range(4)], axis=1)
+            send[peer, 16 * s:16 * s + 16, :] = own[leaf]
             tops.append(own_pts[leaf])
         for p in range(cap // 2):
             both = jnp.where(left8, tops[2 * p], tops[2 * p + 1])
@@ -139,16 +168,17 @@
         return carry
 
     lax.fori_loop(0, n_sub, pack, 0)
-    def value_copy(o):
-        peer = lax.rem(me + o, n_sub)
+
+    def value_copy(k, peer):
         return pltpu.make_async_remote_copy(
-            src_ref=send.at[peer], dst_ref=recv.at[me], send_sem=send_sem.at[o], recv_sem=recv_sem.at[o],
+            src_ref=send.at[peer], dst_ref=recv.at[me], send_sem=send_sem.at[k], recv_sem=recv_sem.at[k],
             device_id={"sub": peer}, device_id_type=MESH)
 
     pl.semaphore_wait(barrier, n_sub - 1 + n_grp - 1)
-    early = n_sub // 2
-    for o in range(1, early):
-        value_copy(o).start()
+    half = n_sub // 2
+    for k in (half, 1):
+        value_copy(k, peers[k]).start()
+    lax.fori_loop(0, 32, turn_basis, 0, unroll=2)
 
     same = (lax.broadcasted_iota(jnp.int32, (256, 256), 0) // 32
             == lax.broadcasted_iota(jnp.int32, (256, 256), 1) // 32)
@@ -156,8 +186,13 @@
     def lift(c, carry):
         first = pl.multiple_of(c * CHILDREN, CHILDREN)
         rows = pl.ds(pl.multiple_of(c * 256, 256), 256)
-        vals = jnp.concatenate([own[first + i] for i in range(CHILDREN)], axis=1)
-        skel = jnp.where(same, mm(basis[rows, :], vals), 0.0)
+        sides = []
+        for side in range(2):
+            four = [own[first + 4 * side + i] for i in range(4)]
+            sides.append(jnp.concatenate([
+                pick_blocks([pltpu.roll(x, 32 * (i - a) % LANES, 1) if i != a else x for i, x in enumerate(four)])
+                for a in range(4)], axis=0))
+        skel = jnp.where(same, mm(basis[rows, :], jnp.concatenate(sides, axis=1)), 0.0)
         up = mm(trans[rows, :], skel, ((0,), (0,)))
         y = up[:, :LANES] + up[:, LANES:]
         y = y + pltpu.roll(y, 64, 1)
@@ -168,30 +203,25 @@
     part = lax.fori_loop(0, par, lift, jnp.zeros((32, LANES), jnp.float32))
     ps_all[me * (par + 1) + par] = dense(part)
 
-    partner = me + 1 - 2 * lax.rem(me, 2)
-
     def skel_copy(whose, to, k):
         part = ps_all.at[pl.ds(whose * (par + 1), par + 1)]
         return pltpu.make_async_remote_copy(
             src_ref=part, dst_ref=part, send_sem=ps_send.at[k], recv_sem=ps_recv.at[k],
             device_id={"sub": to}, device_id_type=MESH)
 
-    def direct(o):
-        return skel_copy(me, lax.rem(me + o, n_sub), o)
-
-    def forward(o):
-        return skel_copy(lax.rem(me + n_sub - o, n_sub), partner, o + 1)
-
-    for o in range(2, n_sub, 2):
-        direct(o).start()
-    skel_copy(me, partner, 1).start()
-    for o in range(early, n_sub):
-        value_copy(o).start()
+    def direct(k):
+        return skel_copy(me, peers[k], k)
+
+    def forward(k):
+        return skel_copy(peers[k], peers[1], k + 1)
+
+    evens = range(n_sub - 2, 0, -2)
+    for k in evens:
+        direct(k).start()
+    direct(1).start()
 
     def keep(l, carry):
-        block = own[l]
-        high = block.astype(jnp.bfloat16).astype(jnp.float32)
-        vals[l] = jnp.concatenate([high, block - high], axis=1).astype(jnp.bfloat16)
+        vals[l] = value_rows(own[l])
         source[l] = source_rows(own_pts[l])
         return carry
 
@@ -199,18 +229,20 @@
         target[l] = target_columns(own_pts[l])
         return carry
 
-    lax.fori_loop(0, par * CHILDREN, keep, 0, unroll=4)
+    lax.fori_loop(0, leaves, keep, 0, unroll=8)
+    for k in evens:
+        direct(k).wait_recv()
+        forward(k).start()
+    for k in list(range(half + 1, n_sub)) + list(range(2, half)):
+        value_copy(k, peers[k]).start()
     vals[slots] = jnp.zeros((64, 64), jnp.bfloat16)
     source[slots] = source_rows(jnp.zeros((8, LANES), jnp.float32))
-    for o in range(2, n_sub, 2):
-        direct(o).wait_recv()
-        forward(o).start()
-    lax.fori_loop(0, par * CHILDREN, keep_target, 0, unroll=4)
-    unpack(cap, par * CHILDREN + me * cap, send.at[me], vals, source)
-    for o in range(2, n_sub, 2):
-        direct(o).wait_send()
-        forward(o).wait()
-    skel_copy(me, partner, 1).wait()
+    lax.fori_loop(0, leaves, keep_target, 0, unroll=8)
+    unpack(cap, leaves + me * cap, send.at[me], vals, source)
+    for k in evens:
+        direct(k).wait_send()
+        forward(k).wait()
+    direct(1).wait()
 
     total = ps_all[par]
     for m in range(1, n_sub):
@@ -259,15 +291,17 @@
 
     lax.fori_loop(0, par, down, 0)
 
-    def arrive(o, carry):
-        value_copy(o).wait_recv()
-        sender = lax.rem(me + n_sub - o, n_sub)
-        unpack(cap, par * CHILDREN + sender * cap, recv.at[sender], vals, source)
-        return carry
-
-    lax.fori_loop(1, n_sub, arrive, 0)
-    for o in range(1, n_sub):
-        value_copy(o).wait_send()
+    def arrive(k, carry):
+        peer = xor(me, k, n_sub)
+        value_copy(k, peer).wait_recv()
+        unpack(cap, leaves + peer * cap, recv.at[peer], vals, source)
+        return carry
+
+    arrive(1, 0)
+    lax.fori_loop(half, n_sub, arrive, 0)
+    lax.fori_loop(2, half, arrive, 0)
+    for k in range(1, n_sub):
+        value_copy(k, peers[k]).wait_send()
 
 
 def near_kernel(leaves, idx, vals, source, target, far, out):
@@ -321,11 +355,8 @@
     near_entries = near_list.shape[0]
     f32 = jnp.float32
 
-    own = jnp.transpose(sources, (2, 1, 0))
     y = jnp.transpose(coords, (2, 0, 1))
     own_pts = jnp.pad(jnp.concatenate([y, y], axis=2), ((0, 0), (0, 5), (0, 0)))
-    basis = jnp.transpose(leaf_basis, (2, 0, 1)).reshape(leaves * 32, 64)
-    trans = jnp.transpose(transfer, (2, 1, 0)).reshape(leaves * 32, 32)
     coup = jnp.transpose(coupling, (0, 2, 3, 1)).reshape(32 * 16 * par, 32)
     gt = jnp.transpose(group_transfer, (0, 2, 1)).reshape(32 * par, 32)
     gcoup = jnp.transpose(group_coupling, (0, 2, 3, 1)).reshape(32 * n_grp * n_grp, 32)
@@ -345,6 +376,10 @@
         in_specs=[smem, smem] + [vmem] * 6 + [pl.BlockSpec(memory_space=pl.ANY)],
         out_specs=(vmem,) * 4,
         scratch_shapes=[
+            pltpu.VMEM((leaves * 16, LANES), f32),
+            pltpu.VMEM((leaves, 16, LANES), f32),
+            pltpu.VMEM((leaves * 32, 64), f32),
+            pltpu.VMEM((leaves * 32, 32), f32),
             pltpu.VMEM((n_sub, rows, LANES), f32),
             pltpu.VMEM((n_sub, rows, LANES), f32),
             pltpu.VMEM((n_sub * (par + 1), 8, LANES), f32),
@@ -355,16 +390,17 @@
             dma((n_sub,)), dma((n_sub,)), dma((n_sub,)), dma((n_sub,)), dma((n_grp,)), dma((n_grp,)), dma,
         ],
         compiler_params=pltpu.CompilerParams(
-            collective_id=0, has_side_effects=True, vmem_limit_bytes=40 * 2**20),
+            collective_id=0, has_side_effects=True, vmem_limit_bytes=34 * 2**20),
         name="exchange_far",
-    )(send_list, far_list, own, own_pts, basis, trans, gt, gcoup, coup)
+    )(send_list, far_list, sources.reshape(32 * 64, leaves), own_pts, leaf_basis.reshape(32 * 64, leaves),
+      transfer.reshape(32 * 32, leaves), gt, gcoup, coup)
 
     out = pl.pallas_call(
         lambda *refs: near_kernel(leaves, *refs),
         out_shape=jax.ShapeDtypeStruct((leaves, 32, 64), f32),
         in_specs=[smem] + [vmem] * 4,
         out_specs=vmem,
-        compiler_params=pltpu.CompilerParams(vmem_limit_bytes=32 * 2**20),
+        compiler_params=pltpu.CompilerParams(vmem_limit_bytes=20 * 2**20),
         name="near_field",
     )(idx, vals, source, target, far.reshape(leaves, 32, 64))
     return jnp.transpose(out, (1, 2, 0))

time: 104 us -> 91.1 us (0.88)
  the two profiles are of different devices: /device:TPU:26 before, /device:TPU:8 now
where the time goes in v4:
time: 91.1 us; the launch traced here: 90.3 us
  Pallas kernels  77.1 us (85%)
  local copies, waits for them, and re-layouts  12.3 us (14%)
    pallas_call x1, Pallas kernels, body(): pl.pallas_call(lambda *refs: exchange_kernel(n_grp, n_sub, par, cap, slot...  60.8 us
    pallas_call x1, Pallas kernels, body(): pl.pallas_call(lambda *refs: near_kernel(leaves, *refs), out_shape=jax.Sh...  16.3 us
    unnamed x17, local copies, waits for them, and re-layouts  9.99 us
    transpose x1, local copies, waits for them, and re-layouts, body(): return jnp.transpose(out, (1, 2, 0))  2.26 us

profile of v4, /device:TPU:8, one launch (start us, length us, event | category | flops | bytes accessed | tf_op | source)
XLA Modules:
  0.0 90.3 jit_solution(17599533423624459410)
XLA Ops:
  0.0 0.7 fusion
  0.7 1.0 %copy.12 = f32[3,64,128]{1,0,2:T(4,128)S(1)} copy(f32[3,64,128]{2,1,0:T(8,128)} %param.12) | data formatting | bytes 196608 | tf_op args[1]
  1.7 0.2 select_maximum_fusion.refs_3_
  2.0 0.0 copy-start
  2.0 2.2 %copy-done = f32[32,32,16,16]{1,3,2,0:T(8,128)S(1)} copy-done((f32[32,32,16,16]{1,3,2,0:T(8,128)S(1)}, f32[32,32,16,16]{1,3,2,0:T(8,128)}, u32[]{:S(2)}) %copy-start) | copy-done | bytes 1048600
  4.1 0.0 copy-start.1
  4.1 1.2 %copy-done.1 = f32[32,64,128]{2,1,0:T(8,128)S(1)} copy-done((f32[32,64,128]{2,1,0:T(8,128)S(1)}, f32[32,64,128]{2,1,0:T(8,128)}, u32[]{:S(2)}) %copy-start.1) | copy-done | bytes 1048600
  5.4 0.0 copy-start.2
  5.4 1.2 %copy-done.2 = f32[32,64,128]{2,1,0:T(8,128)S(1)} copy-done((f32[32,64,128]{2,1,0:T(8,128)S(1)}, f32[32,64,128]{2,1,0:T(8,128)}, u32[]{:S(2)}) %copy-start.2) | copy-done | bytes 1048600
  6.6 0.0 copy-start.3
  6.6 1.0 %copy-done.3 = f32[32,32,128]{2,1,0:T(8,128)S(1)} copy-done((f32[32,32,128]{2,1,0:T(8,128)S(1)}, f32[32,32,128]{2,1,0:T(8,128)}, u32[]{:S(2)}) %copy-start.3) | copy-done | bytes 524312
  7.6 0.0 copy-start.4
  7.6 0.9 %copy-done.4 = f32[32,32,16]{1,2,0:T(8,128)S(1)} copy-done((f32[32,32,16]{1,2,0:T(8,128)S(1)}, f32[32,32,16]{1,2,0:T(8,128)}, u32[]{:S(2)}) %copy-start.4) | copy-done | bytes 65560
  8.6 0.0 copy-start.5
  8.6 0.9 %copy-done.5 = f32[32,32,4,4]{1,3,2,0:T(4,128)S(1)} copy-done((f32[32,32,4,4]{1,3,2,0:T(4,128)S(1)}, f32[32,32,4,4]{1,3,2,0:T(4,128)}, u32[]{:S(2)}) %copy-start.5) | copy-done | bytes 65560
  9.5 0.0 copy-start.6
  9.5 0.7 copy-done.6
  10.2 0.0 copy-start.7
  10.2 0.7 copy-done.7
  10.9 60.8 %exchange_far.1 = (bf16[257,64,64]{2,1,0:T(8,128)(2,1)S(1)}, bf16[257,48,128]{2,1,0:T(8,128)(2,1)S(1)}, bf16[128,64,48]{2,1,0:T(8,128)(2,1)S(1)}, f32[4096,64]{1,0:T(8,128)S(1)}) custom-call(s32[8,16]{1,0:T(8,128)S(1)} %copy-done.7, s32[16,16]{1,0:T(8,128)S(1)} %copy-done.6, f32[2048,128]{1,0:T(8,128)S(1)} %bitcast.18, ...), custom_call_target="tpu_custom_call" | custom-call | tf_op jit(solution)/shard_map/exchange_far/pallas_call | solution.py:370
  71.7 16.3 %near_field.1 = f32[128,32,64]{2,1,0:T(8,128)S(1)} custom-call(s32[8,128]{1,0:T(8,128)S(1)} %pad.8.refs_0_, bf16[257,64,64]{2,1,0:T(8,128)(2,1)S(1)} %get-tuple-element.9.refs_1_, bf16[257,48,128]{2,1,0:T(8,128)(2,1)S(1)} %get-tuple-element.10.refs_2_, bf16[128,64,48]{2,1,0:T(8,128)(2,1)S(1)} %get-tuple-element.11.refs_3_, f32[128,32,64]{2,1,0:T(8,128)S(1)} %bitcast.17), custom_call_target="tpu_custom_call" | custom-call | tf_op jit(solution)/shard_map/near_field/pallas_call | solution.py:398
  88.0 2.3 %copy.13 = f32[32,64,128]{2,1,0:T(8,128)} copy(f32[32,64,128]{1,0,2:T(8,128)S(1)} %bitcast.15) | data formatting | bytes 2097152 | tf_op jit(solution)/shard_map/transpose | solution.py:406
  (1 shorter events, 0.0 us)
Async XLA Ops:
  2.0 2.2 %copy-start = (f32[32,32,16,16]{1,3,2,0:T(8,128)S(1)}, f32[32,32,16,16]{1,3,2,0:T(8,128)}, u32[]{:S(2)}) copy-start(f32[32,32,16,16]{1,3,2,0:T(8,128)} %param.19) | copy-start | bytes 3145732
  4.1 1.2 %copy-start.1 = (f32[32,64,128]{2,1,0:T(8,128)S(1)}, f32[32,64,128]{2,1,0:T(8,128)}, u32[]{:S(2)}) copy-start(f32[32,64,128]{2,1,0:T(8,128)} %param.11) | copy-start | bytes 3145732
  5.4 1.2 %copy-start.2 = (f32[32,64,128]{2,1,0:T(8,128)S(1)}, f32[32,64,128]{2,1,0:T(8,128)}, u32[]{:S(2)}) copy-start(f32[32,64,128]{2,1,0:T(8,128)} %param.13) | copy-start | bytes 3145732
  6.6 1.0 %copy-start.3 = (f32[32,32,128]{2,1,0:T(8,128)S(1)}, f32[32,32,128]{2,1,0:T(8,128)}, u32[]{:S(2)}) copy-start(f32[32,32,128]{2,1,0:T(8,128)} %param.14) | copy-start | bytes 1572868
  7.6 0.9 %copy-start.4 = (f32[32,32,16]{1,2,0:T(8,128)S(1)}, f32[32,32,16]{1,2,0:T(8,128)}, u32[]{:S(2)}) copy-start(f32[32,32,16]{1,2,0:T(8,128)} %param.20) | copy-start | bytes 196612
  8.6 0.9 %copy-start.5 = (f32[32,32,4,4]{1,3,2,0:T(4,128)S(1)}, f32[32,32,4,4]{1,3,2,0:T(4,128)}, u32[]{:S(2)}) copy-start(f32[32,32,4,4]{1,3,2,0:T(4,128)} %param.21) | copy-start | bytes 196612
  9.5 0.7 copy-start.6
  10.2 0.7 copy-start.7

commit v5 on v4

--- a/solution.py
+++ b/solution.py
@@ -12,7 +12,8 @@
 MESH = pl.DeviceIdType.MESH
 LANES = 128
 CHILDREN = 8
-TOGETHER = 4
+TOGETHER = 8
+STAGE = 4
 
 
 def halves(x):
@@ -105,24 +106,28 @@
 def unpack(cap, base, got, vals, source):
     left8 = lax.broadcasted_iota(jnp.int32, (8, LANES), 1) < 64
     row = lax.broadcasted_iota(jnp.int32, (8, LANES), 0)
+    tables = [value_rows(got[16 * s:16 * s + 16, :]) for s in range(cap)]
     for s in range(cap):
-        vals[base + s] = value_rows(got[16 * s:16 * s + 16, :])
+        vals[base + s] = tables[s]
     tiles = []
     for d in range(3):
         start = 16 * cap + (cap // 2) * d
         tile = got[start:start + cap // 2, :]
         turned = pltpu.roll(tile, 64, 1)
         tiles.append((jnp.where(left8, tile, turned), jnp.where(left8, turned, tile)))
+    tables = []
     for s in range(cap):
         parts = [jnp.broadcast_to(t[s % 2][s // 2:s // 2 + 1], (8, LANES)) for t in tiles]
-        source[base + s] = source_rows(jnp.where(row == 0, parts[0], jnp.where(row == 1, parts[1], parts[2])))
+        tables.append(source_rows(jnp.where(row == 0, parts[0], jnp.where(row == 1, parts[1], parts[2]))))
+    for s in range(cap):
+        source[base + s] = tables[s]
 
 
 def exchange_kernel(n_grp, n_sub, par, cap, slots,
-                    send_list, far_list, src, own_pts, raw_basis, raw_trans, gt, gcoup, coup_hbm,
-                    vals, source, target, far,
-                    flat, own, basis, trans, send, recv, ps_all, gs_all, loose_all, field, coup, send_sem, recv_sem, ps_send, ps_recv, gs_send,
-                    gs_recv, coup_sem):
+                    send_list, far_list, idx, own_pts, src_hbm, basis_hbm, trans_hbm, gt_hbm, gcoup_hbm, coup_hbm,
+                    out,
+                    vals, source, target, far, src, raw_basis, raw_trans, gt, gcoup, flat, own, basis, trans, send, recv, ps_all, gs_all, loose_all, field, coup, send_sem, recv_sem, ps_send, ps_recv, gs_send,
+                    gs_recv, load_sem):
     me = lax.axis_index("sub")
     grp = lax.axis_index("grp")
     barrier = pltpu.get_barrier_semaphore()
@@ -132,34 +137,45 @@
     for o in range(1, n_grp):
         pl.semaphore_signal(barrier, inc=1, device_id={"grp": lax.rem(grp + o, n_grp)}, device_id_type=MESH)
 
-    coup_copy = pltpu.make_async_copy(coup_hbm, coup, coup_sem)
-    coup_copy.start()
+    loads = [pltpu.make_async_copy(there, here, load_sem.at[n]) for n, (there, here) in enumerate([
+        (src_hbm, src), (basis_hbm, raw_basis), (trans_hbm, raw_trans), (gt_hbm, gt), (gcoup_hbm, gcoup),
+        (coup_hbm, coup)])]
+    for load in loads:
+        load.start()
     leaves = par * CHILDREN
 
-    def turn_sources(q, carry):
-        cols = jnp.concatenate([src[pl.ds(16 * a + q, 32, stride=64), :] for a in range(4)], axis=0)
-        flat[pl.ds(q, leaves, stride=16), :] = cols.T
-        return carry
-
-    def turn_basis(k, carry):
-        basis[pl.ds(k, leaves, stride=32), :] = raw_basis[pl.ds(pl.multiple_of(64 * k, 64), 64), :].T
-        trans[pl.ds(k, leaves, stride=32), :] = raw_trans[pl.ds(k, 32, stride=32), :].T
-        return carry
-
-    def own_copy(l, carry):
-        own[l] = flat[pl.ds(pl.multiple_of(16 * l, 16), 16), :]
-        return carry
-
-    lax.fori_loop(0, 16, turn_sources, 0, unroll=2)
-    lax.fori_loop(0, leaves, own_copy, 0, unroll=16)
+    def turn_sources(step, carry):
+        qs = [STAGE * step + n for n in range(STAGE)]
+        cols = [jnp.concatenate([src[pl.ds(16 * a + q, 32, stride=64), :] for a in range(4)], axis=0).T for q in qs]
+        for q, col in zip(qs, cols):
+            flat[pl.ds(q, leaves, stride=16), :] = col
+        return carry
+
+    def turn_basis(step, carry):
+        ks = [STAGE * step + n for n in range(STAGE)]
+        turned = [raw_basis[pl.ds(pl.multiple_of(64 * k, 64), 64), :].T for k in ks]
+        moved = [raw_trans[pl.ds(k, 32, stride=32), :].T for k in ks]
+        for k, b, t in zip(ks, turned, moved):
+            basis[pl.ds(k, leaves, stride=32), :] = b
+            trans[pl.ds(k, leaves, stride=32), :] = t
+        return carry
+
+    def own_copy(step, carry):
+        rows = flat[pl.ds(pl.multiple_of(256 * step, 256), 256), :]
+        own[pl.ds(pl.multiple_of(16 * step, 16), 16)] = rows.reshape(16, 16, LANES)
+        return carry
+
+    loads[0].wait()
+    lax.fori_loop(0, 16 // STAGE, turn_sources, 0)
+    lax.fori_loop(0, leaves // 16, own_copy, 0)
     left8 = lax.broadcasted_iota(jnp.int32, (8, LANES), 1) < 64
 
     def pack(peer, carry):
-        tops = []
+        chosen = [send_list[peer, s] for s in range(cap)]
+        blocks = [own[leaf] for leaf in chosen]
+        tops = [own_pts[leaf] for leaf in chosen]
         for s in range(cap):
-            leaf = send_list[peer, s]
-            send[peer, 16 * s:16 * s + 16, :] = own[leaf]
-            tops.append(own_pts[leaf])
+            send[peer, 16 * s:16 * s + 16, :] = blocks[s]
         for p in range(cap // 2):
             both = jnp.where(left8, tops[2 * p], tops[2 * p + 1])
             for d in range(3):
@@ -178,29 +194,39 @@
     half = n_sub // 2
     for k in (half, 1):
         value_copy(k, peers[k]).start()
-    lax.fori_loop(0, 32, turn_basis, 0, unroll=2)
+    for load in loads[1:4]:
+        load.wait()
+    lax.fori_loop(0, 32 // STAGE, turn_basis, 0)
 
     same = (lax.broadcasted_iota(jnp.int32, (256, 256), 0) // 32
             == lax.broadcasted_iota(jnp.int32, (256, 256), 1) // 32)
 
-    def lift(c, carry):
-        first = pl.multiple_of(c * CHILDREN, CHILDREN)
-        rows = pl.ds(pl.multiple_of(c * 256, 256), 256)
+    def rows_of(c):
+        return pl.ds(pl.multiple_of(c * 256, 256), 256)
+
+    def columns(c):
         sides = []
         for side in range(2):
-            four = [own[first + 4 * side + i] for i in range(4)]
+            four = [own[c * CHILDREN + 4 * side + i] for i in range(4)]
             sides.append(jnp.concatenate([
                 pick_blocks([pltpu.roll(x, 32 * (i - a) % LANES, 1) if i != a else x for i, x in enumerate(four)])
                 for a in range(4)], axis=0))
-        skel = jnp.where(same, mm(basis[rows, :], jnp.concatenate(sides, axis=1)), 0.0)
-        up = mm(trans[rows, :], skel, ((0,), (0,)))
-        y = up[:, :LANES] + up[:, LANES:]
-        y = y + pltpu.roll(y, 64, 1)
-        y = y + pltpu.roll(y, 32, 1)
-        ps_all[me * (par + 1) + c] = dense(y)
-        return carry + mm(gt[pl.ds(c, 32, stride=par), :], y)
-
-    part = lax.fori_loop(0, par, lift, jnp.zeros((32, LANES), jnp.float32))
+        return jnp.concatenate(sides, axis=1)
+
+    def lift(step, carry):
+        cs = [STAGE * step + n for n in range(STAGE)]
+        sides = [columns(c) for c in cs]
+        skels = [jnp.where(same, mm(basis[rows_of(c), :], v), 0.0) for c, v in zip(cs, sides)]
+        ups = [mm(trans[rows_of(c), :], skel, ((0,), (0,))) for c, skel in zip(cs, skels)]
+        ys = [up[:, :LANES] + up[:, LANES:] for up in ups]
+        ys = [y + pltpu.roll(y, 64, 1) for y in ys]
+        ys = [y + pltpu.roll(y, 32, 1) for y in ys]
+        parts = [mm(gt[pl.ds(c, 32, stride=par), :], y) for c, y in zip(cs, ys)]
+        for c, y in zip(cs, ys):
+            ps_all[me * (par + 1) + c] = dense(y)
+        return carry + sum(parts)
+
+    part = lax.fori_loop(0, par // STAGE, lift, jnp.zeros((32, LANES), jnp.float32))
     ps_all[me * (par + 1) + par] = dense(part)
 
     def skel_copy(whose, to, k):
@@ -220,16 +246,23 @@
         direct(k).start()
     direct(1).start()
 
-    def keep(l, carry):
-        vals[l] = value_rows(own[l])
-        source[l] = source_rows(own_pts[l])
-        return carry
-
-    def keep_target(l, carry):
-        target[l] = target_columns(own_pts[l])
-        return carry
-
-    lax.fori_loop(0, leaves, keep, 0, unroll=8)
+    def keep(step, carry):
+        ls = [8 * step + n for n in range(8)]
+        values = [value_rows(own[l]) for l in ls]
+        points = [source_rows(own_pts[l]) for l in ls]
+        for l, v, p in zip(ls, values, points):
+            vals[l] = v
+            source[l] = p
+        return carry
+
+    def keep_target(step, carry):
+        ls = [8 * step + n for n in range(8)]
+        points = [target_columns(own_pts[l]) for l in ls]
+        for l, p in zip(ls, points):
+            target[l] = p
+        return carry
+
+    lax.fori_loop(0, leaves // 8, keep, 0)
     for k in evens:
         direct(k).wait_recv()
         forward(k).start()
@@ -237,7 +270,7 @@
         value_copy(k, peers[k]).start()
     vals[slots] = jnp.zeros((64, 64), jnp.bfloat16)
     source[slots] = source_rows(jnp.zeros((8, LANES), jnp.float32))
-    lax.fori_loop(0, leaves, keep_target, 0, unroll=8)
+    lax.fori_loop(0, leaves // 8, keep_target, 0)
     unpack(cap, leaves + me * cap, send.at[me], vals, source)
     for k in evens:
         direct(k).wait_send()
@@ -263,15 +296,22 @@
         return carry
 
     lax.fori_loop(0, n_sub, loosen, 0)
-    coup_copy.wait()
-
-    def local(c, carry):
-        partners = jnp.concatenate([loose_all[far_list[f, c]] for f in range(16)], axis=0)
-        blocks = jnp.concatenate([coup[pl.ds(f * par + c, 32, stride=16 * par), :] for f in range(16)], axis=1)
-        field[c] = spread_lanes(mm(blocks, partners))
-        return carry
-
-    lax.fori_loop(0, par, local, 0)
+    for load in loads[4:]:
+        load.wait()
+
+    def local(step, carry):
+        cs = [STAGE * step + n for n in range(STAGE)]
+        sums = []
+        for c in cs:
+            partners = jnp.concatenate([loose_all[far_list[f, c]] for f in range(16)], axis=0)
+            blocks = jnp.concatenate([coup[pl.ds(f * par + c, 32, stride=16 * par), :] for f in range(16)], axis=1)
+            sums.append(mm(blocks, partners))
+        sums = [spread_lanes(x) for x in sums]
+        for c, x in zip(cs, sums):
+            field[c] = x
+        return carry
+
+    lax.fori_loop(0, par // STAGE, local, 0)
     for o in range(1, n_grp):
         group_copy(o).wait()
     inflow = jnp.zeros((32, LANES), jnp.float32)
@@ -281,15 +321,17 @@
         inflow = inflow + mm(block * live, loose(gs_all[h]))
     inflow = spread_lanes(inflow)
 
-    def down(c, carry):
-        rows = pl.ds(pl.multiple_of(c * 256, 256), 256)
-        here = field[c] + mm(gt[pl.ds(c, 32, stride=par), :], inflow, ((0,), (0,)))
-        leaf_field = mm(here.T, trans[rows, :], ((1,), (1,)))
-        spread = jnp.where(same, jnp.concatenate([leaf_field, leaf_field], axis=0), 0.0)
-        far[rows, :] = mm(spread, basis[rows, :])
-        return carry
-
-    lax.fori_loop(0, par, down, 0)
+    def down(step, carry):
+        cs = [STAGE * step + n for n in range(STAGE)]
+        here = [(field[c] + mm(gt[pl.ds(c, 32, stride=par), :], inflow, ((0,), (0,)))).T for c in cs]
+        leaf_fields = [mm(x, trans[rows_of(c), :], ((1,), (1,))) for c, x in zip(cs, here)]
+        spreads = [jnp.where(same, jnp.concatenate([x, x], axis=0), 0.0) for x in leaf_fields]
+        results = [mm(x, basis[rows_of(c), :]) for c, x in zip(cs, spreads)]
+        for c, x in zip(cs, results):
+            far[rows_of(c), :] = x
+        return carry
+
+    lax.fori_loop(0, par // STAGE, down, 0)
 
     def arrive(k, carry):
         peer = xor(me, k, n_sub)
@@ -302,9 +344,10 @@
     lax.fori_loop(2, half, arrive, 0)
     for k in range(1, n_sub):
         value_copy(k, peers[k]).wait_send()
-
-
-def near_kernel(leaves, idx, vals, source, target, far, out):
+    near_field(leaves, idx, vals, source, target, far, out)
+
+
+def near_field(leaves, idx, vals, source, target, far, out):
     left48 = lax.broadcasted_iota(jnp.int32, (48, LANES), 1) < 64
     first64 = lax.broadcasted_iota(jnp.int32, (64, 64), 1) < 32
 
@@ -327,7 +370,7 @@
             fulls.append(jnp.dot(side, values, preferred_element_type=jnp.float32))
         nears = [(full[:64] + jnp.where(first64, full[64:], 0.0)).T for full in fulls]
         for i, near in zip(ids, nears):
-            out[i] = far[i] + INV_FOUR_PI * (near[:32] + near[32:])
+            out[i] = far[pl.ds(pl.multiple_of(32 * i, 32), 32), :] + INV_FOUR_PI * (near[:32] + near[32:])
         return carry
 
     lax.fori_loop(0, leaves // TOGETHER, some_leaves, 0)
@@ -367,15 +410,21 @@
     smem = pl.BlockSpec(memory_space=pltpu.SMEM)
     rows = 16 * cap + 3 * (cap // 2)
     dma = pltpu.SemaphoreType.DMA
-    vals, source, target, far = pl.pallas_call(
+    out = pl.pallas_call(
         lambda *refs: exchange_kernel(n_grp, n_sub, par, cap, slots, *refs),
-        out_shape=(jax.ShapeDtypeStruct((slots + 1, 64, 64), jnp.bfloat16),
-                   jax.ShapeDtypeStruct((slots + 1, 48, LANES), jnp.bfloat16),
-                   jax.ShapeDtypeStruct((leaves, 64, 48), jnp.bfloat16),
-                   jax.ShapeDtypeStruct((leaves * 32, 64), f32)),
-        in_specs=[smem, smem] + [vmem] * 6 + [pl.BlockSpec(memory_space=pl.ANY)],
-        out_specs=(vmem,) * 4,
+        out_shape=jax.ShapeDtypeStruct((leaves, 32, 64), f32),
+        in_specs=[smem, smem, smem, vmem] + [pl.BlockSpec(memory_space=pltpu.HBM)] * 6,
+        out_specs=vmem,
         scratch_shapes=[
+            pltpu.VMEM((slots + 1, 64, 64), jnp.bfloat16),
+            pltpu.VMEM((slots + 1, 48, LANES), jnp.bfloat16),
+            pltpu.VMEM((leaves, 64, 48), jnp.bfloat16),
+            pltpu.VMEM((leaves * 32, 64), f32),
+            pltpu.VMEM((32 * 64, leaves), f32),
+            pltpu.VMEM((32 * 64, leaves), f32),
+            pltpu.VMEM((32 * 32, leaves), f32),
+            pltpu.VMEM((32 * par, 32), f32),
+            pltpu.VMEM((32 * n_grp * n_grp, 32), f32),
             pltpu.VMEM((leaves * 16, LANES), f32),
             pltpu.VMEM((leaves, 16, LANES), f32),
             pltpu.VMEM((leaves * 32, 64), f32),
@@ -387,22 +436,14 @@
             pltpu.VMEM((n_sub * par, 32, LANES), f32),
             pltpu.VMEM((par, 32, LANES), f32),
             pltpu.VMEM((32 * 16 * par, 32), f32),
-            dma((n_sub,)), dma((n_sub,)), dma((n_sub,)), dma((n_sub,)), dma((n_grp,)), dma((n_grp,)), dma,
+            dma((n_sub,)), dma((n_sub,)), dma((n_sub,)), dma((n_sub,)), dma((n_grp,)), dma((n_grp,)), dma((6,)),
         ],
         compiler_params=pltpu.CompilerParams(
-            collective_id=0, has_side_effects=True, vmem_limit_bytes=34 * 2**20),
-        name="exchange_far",
-    )(send_list, far_list, sources.reshape(32 * 64, leaves), own_pts, leaf_basis.reshape(32 * 64, leaves),
+            collective_id=0, has_side_effects=True, vmem_limit_bytes=56 * 2**20),
+        name="whole_step",
+    )(send_list, far_list, idx, own_pts, sources.reshape(32 * 64, leaves), leaf_basis.reshape(32 * 64, leaves),
       transfer.reshape(32 * 32, leaves), gt, gcoup, coup)
 
-    out = pl.pallas_call(
-        lambda *refs: near_kernel(leaves, *refs),
-        out_shape=jax.ShapeDtypeStruct((leaves, 32, 64), f32),
-        in_specs=[smem] + [vmem] * 4,
-        out_specs=vmem,
-        compiler_params=pltpu.CompilerParams(vmem_limit_bytes=20 * 2**20),
-        name="near_field",
-    )(idx, vals, source, target, far.reshape(leaves, 32, 64))
     return jnp.transpose(out, (1, 2, 0))
 
 

time: 91.1 us -> 60.7 us (0.67)
  Pallas kernels: 77.1 us -> 53.5 us
  local copies, waits for them, and re-layouts: 12.3 us -> 5.27 us
    pallas_call x1 -> x0, Pallas kernels: 16.3 us -> none  [body(): pl.pallas_call(lambda *refs: near_kernel(leaves, *refs), out_shape=jax.Sh...]
    unnamed x17 -> x1, local copies, waits for them, and re-layouts: 9.99 us -> 1.04 us
    pallas_call x1, Pallas kernels: 60.8 us -> 53.5 us  [body(): pl.pallas_call(lambda *refs: exchange_kernel(n_grp, n_sub, par, cap, slot...]
    transpose x1, local copies, waits for them, and re-layouts: 2.26 us -> 3.63 us  [body(): return jnp.transpose(out, (1, 2, 0))]
where the time goes in v5:
time: 60.7 us; the launch traced here: 60.5 us
  Pallas kernels  53.5 us (88%)
  local copies, waits for them, and re-layouts  5.27 us (9%)
  other arithmetic  1.69 us (3%)
    pallas_call x1, Pallas kernels, body(): pl.pallas_call(lambda *refs: exchange_kernel(n_grp, n_sub, par, cap, slot...  53.5 us
    transpose x1, local copies, waits for them, and re-layouts, body(): return jnp.transpose(out, (1, 2, 0))  3.63 us

profile of v5, /device:TPU:8, one launch (start us, length us, event | category | flops | bytes accessed | tf_op | source)
XLA Modules:
  0.0 60.5 jit_solution(4090561208630770608)
XLA Ops:
  0.0 0.7 %fusion = s32[7,128]{1,0:T(8,128)S(1)} fusion(s32[7,128]{1,0:T(8,128)} %param.16, s32[128]{0:T(128)} %param.17), kind=kLoop, calls=%fused_computation.3 | loop fusion | flops 1792 | bytes 7680 | tf_op jit(solution)/shard_map/jit(_where)/select_n | solution.py:407
  0.7 0.6 pad.8.refs_2_
  1.3 1.0 %copy.12 = f32[3,64,128]{1,0,2:T(4,128)S(1)} copy(f32[3,64,128]{2,1,0:T(8,128)} %param.12) | data formatting | bytes 196608 | tf_op args[1]
  2.3 1.0 %select_maximum_fusion.refs_3_ = f32[128,8,128]{2,1,0:T(8,128)} fusion(f32[128,3,64]{2,1,0:T(4,128)S(1)} %bitcast.18), kind=kLoop, calls=%fused_computation | loop fusion | flops 524288 | bytes 622592 | tf_op jit(solution)/shard_map/concatenate | solution.py:402
  3.3 53.5 %whole_step.1 = f32[128,32,64]{2,1,0:T(8,128)} custom-call(s32[8,16]{1,0:T(8,128)} %refs_0_.1, s32[16,16]{1,0:T(8,128)} %refs_1_.1, s32[8,128]{1,0:T(8,128)} %pad.8.refs_2_, f32[128,8,128]{2,1,0:T(8,128)} %select_maximum_fusion.refs_3_, f32[2048,128]{1,0:T(8,128)} %bitcast.16, f32[2048,128]{1,0:T(8,128)} %bitcast.17, f32[1024,128]{1,0:T(8,128)} %bitcast.19, ...), custom_call_target="tpu_custom_call" | custom-call | tf_op jit(solution)/shard_map/whole_step/pallas_call | solution.py:413
  56.8 3.6 %copy.13 = f32[32,64,128]{2,1,0:T(8,128)} copy(f32[32,64,128]{1,0,2:T(8,128)} %bitcast.14) | data formatting | bytes 2097152 | tf_op jit(solution)/shard_map/transpose | solution.py:447
